TPU v7x, 512 devices: a whole 4x4x16 slice. The times are simulated.
512 devices in a mesh: pipe: 32 (over y_lo, z), tensor: 16 (over x, y_hi, core).
Axes of the slice: x: 4, y: 4 (y_hi: 2, y_lo: 2; y = y_hi * 2 + y_lo), z: 16, core: 2. Of those that a mesh axis runs over, the one named last changes fastest.
Arguments:
- activations: bfloat16 [32, 256, 4096], P('pipe', 'tensor'), may hold values from -6 to 6
- hidden_grad: bfloat16 [32, 256, 14336], P('pipe', None, 'tensor'), may hold values from -0.375 to 0.375
- residual_grad: bfloat16 [32, 256, 4096], P('pipe', 'tensor'), may hold values from -0.59765625 to 0.59765625
- weight_tiles: bfloat16 [32, 16, 64, 128, 128], P('pipe', 'tensor'), may hold values from -0.1875 to 0.1875
- tile_ids: int32 [32, 16, 64], P('pipe', 'tensor'), may hold values from 0 to 223, as said below
- tile_counts: int32 [32, 16], P('pipe', 'tensor'), may hold values from 16 to 64, as said below
Outputs:
- received: bfloat16 [32, 256, 4096], P('pipe', 'tensor')
- weight_grads: bfloat16 [32, 16, 64, 128, 128], P('pipe', 'tensor')
Inputs may be any that keep to these rules, and one draw needn't show every extreme that they name: `tile_ids`: within each shard's list the entries are distinct and increasing; entries at slots from that shard's count on are not read. `tile_counts`: in every section some shard has exactly 64 tiles.
All inputs are finite; a program needn't handle non-finite values.
Results may differ from a plain program's by a relative error of at most 0.001.
Values may be sent and summed in bfloat16 or wider, within the bound.
No kernel may reach another device: no remote copies, remote signals or barrier semaphores. Data moves between devices by JAX's collectives and lax.ppermute only.
A program may use at most 64 MiB of HBM per device.

v0:
```python
import jax
import jax.numpy as jnp
from jax import lax
from jax.sharding import PartitionSpec as P


def passed_along(x, axis, by):
    count = lax.axis_size(axis)
    pairs = [(i, i + by) for i in range(count) if 0 <= i + by < count]
    return lax.ppermute(x, axis, pairs)


def sweep(partial_value, tile_set, tile_names, hidden_blocks, act_blocks, lower_slot, upper_slot):
    slot_total = tile_set.shape[0]
    blocks_d = tile_width_blocks(act_blocks)
    grad_tiles = jnp.zeros(tile_set.shape, jnp.bfloat16)
    turn_count = jnp.maximum(upper_slot - lower_slot + 7, 0) // 8

    def advance(turn_index, carried):
        partial_value, grad_tiles = carried
        begin_at = lower_slot + 8 * turn_index
        first_slot = jnp.minimum(begin_at, slot_total - 8)
        slot_index = first_slot + jnp.arange(8, dtype=jnp.int32)
        usable = (slot_index >= begin_at) & (slot_index < upper_slot)
        group_names = lax.dynamic_slice_in_dim(tile_names, first_slot, 8, 0)
        hidden_block = group_names // blocks_d
        model_block = group_names % blocks_d
        grad_part = jnp.take(hidden_blocks, hidden_block, axis=1)
        tile_group = lax.dynamic_slice_in_dim(tile_set, first_slot, 8, 0)
        backward = jnp.einsum(
            "tsk,sjk->tsj", grad_part, tile_group, preferred_element_type=jnp.float32
        )
        backward = jnp.where(usable[None, :, None], backward, 0.0)
        partial_value = partial_value.at[:, model_block].add(backward)
        act_part = jnp.take(act_blocks, model_block, axis=1)
        fresh_grads = jnp.einsum(
            "tsj,tsk->sjk", act_part, grad_part, preferred_element_type=jnp.float32
        ).astype(jnp.bfloat16)
        held_grads = lax.dynamic_slice_in_dim(grad_tiles, first_slot, 8, 0)
        merged = jnp.where(usable[:, None, None], fresh_grads, held_grads)
        grad_tiles = lax.dynamic_update_slice_in_dim(grad_tiles, merged, first_slot, 0)
        return (partial_value, grad_tiles)

    return lax.fori_loop(0, turn_count, advance, (partial_value, grad_tiles))


def tile_width_blocks(act_blocks):
    return act_blocks.shape[1]


def shards(activations, hidden_grad, residual_grad, weight_tiles, tile_ids, tile_counts):
    gathered = lax.all_gather(activations[0], "tensor", axis=0, tiled=True)
    token_total = gathered.shape[0]
    model_width = gathered.shape[1]
    tile_width = weight_tiles.shape[-1]
    blocks_d = model_width // tile_width
    act_blocks = gathered.reshape(token_total, blocks_d, tile_width)
    own_hidden = hidden_grad[0].reshape(token_total, -1, tile_width)
    tile_set = weight_tiles[0, 0]
    tile_names = tile_ids[0, 0]
    live_count = tile_counts[0, 0]
    work_list = (tile_set, tile_names, own_hidden, 0, live_count)
    partial_value = jnp.zeros((token_total, blocks_d, tile_width), jnp.float32)
    tiles_here, names_here, hidden_here, lower, upper = work_list
    partial_value, grads_here = sweep(
        partial_value, tiles_here, names_here, hidden_here, act_blocks, lower, upper
    )
    reduced = lax.psum_scatter(
        partial_value.reshape(token_total, model_width), "tensor", scatter_dimension=0, tiled=True
    )
    sent_grad = (residual_grad[0].astype(jnp.float32) + reduced).astype(jnp.bfloat16)
    received = passed_along(sent_grad, "pipe", -1)
    return (received[None], grads_here[None, None])


def solution(mesh):
    return jax.shard_map(
        shards,
        mesh=mesh,
        in_specs=(
            P("pipe", "tensor", None),
            P("pipe", None, "tensor"),
            P("pipe", "tensor", None),
            P("pipe", "tensor", None, None, None),
            P("pipe", "tensor", None),
            P("pipe", "tensor"),
        ),
        out_specs=(P("pipe", "tensor", None), P("pipe", "tensor", None, None, None)),
        check_vma=False,
    )
```

profile of v0, /device:TPU:8, one launch (start us, length us, event | category | flops | bytes accessed | tf_op | source)
XLA Modules:
  0.0 307.7 jit_solution(1656422119678822781)
XLA Ops:
  10.1 68.4 %all-gather.3.cloned.1.call-done = bf16[1,256,4096]{2,1,0:T(8,128)(2,1)} async-done(((bf16[1,16,4096]{2,1,0:T(8,128)(2,1)}), bf16[1,256,4096]{2,1,0:T(8,128)(2,1)}) %all-gather.3.cloned.1.call-update) | async-done | bytes 2097168 | tf_op jit(solution)/shard_map/all_gather | solution.py:52
  78.5 3.3 %copy.28 = bf16[1,256,4096]{1,2,0:T(8,128)(2,1)S(1)} copy(bf16[1,256,4096]{2,1,0:T(8,128)(2,1)} %all-gather.3.cloned.1.call-done) | data formatting | bytes 4194304 | tf_op jit(solution)/shard_map/all_gather | solution.py:52
  81.8 2.9 copy.30
  86.5 2.5 broadcast_in_dim.83
  89.0 70.7 %while.14 = (s32[]{:T(128)}, f32[256,32,128]{2,0,1:T(8,128)}, bf16[64,128,128]{2,1,0:T(8,128)(2,1)}, s32[]{:T(128)}, s32[64]{0:T(128)S(1)}, /*index=5*/s32[]{:T(...) while((s32[]{:T(128)}, f32[256,32,128]{2,0,1:T(8,128)}, ...), condition=%wide.region_2.3_spmd, body=%wide.region_0.2_spmd.sunk | while | flops 135792960 | bytes 10756731 | solution.py:44
  90.5 3.0 gather_fusion.1
  95.2 2.2 fusion.26
  97.4 3.3 %scatter_fusion = f32[256,32,128]{2,0,1:T(8,128)} fusion(f32[256,32,128]{2,0,1:T(8,128)} %get-tuple-element.258, s32[8]{0:T(128)S(1)} %get-tuple-element.237, f32[8,256,128]{2,1,0:T(8,128)S(1)} %copy.36), kind=kCustom, calls=%fused_computation.2.clone.1 | custom fusion | flops 262144 | bytes 3145760 | tf_op jit(solution)/shard_map/while/body/scatter-add | solution.py:34
  102.3 3.0 gather_fusion.1
  107.0 2.2 fusion.26
  109.2 3.4 %scatter_fusion = f32[256,32,128]{2,0,1:T(8,128)} fusion(f32[256,32,128]{2,0,1:T(8,128)} %get-tuple-element.258, s32[8]{0:T(128)S(1)} %get-tuple-element.237, f32[8,256,128]{2,1,0:T(8,128)S(1)} %copy.36), kind=kCustom, calls=%fused_computation.2.clone.1 | custom fusion | flops 262144 | bytes 3145760 | tf_op jit(solution)/shard_map/while/body/scatter-add | solution.py:34
  114.1 3.0 gather_fusion.1
  118.8 2.2 fusion.26
  121.0 3.3 %scatter_fusion = f32[256,32,128]{2,0,1:T(8,128)} fusion(f32[256,32,128]{2,0,1:T(8,128)} %get-tuple-element.258, s32[8]{0:T(128)S(1)} %get-tuple-element.237, f32[8,256,128]{2,1,0:T(8,128)S(1)} %copy.36), kind=kCustom, calls=%fused_computation.2.clone.1 | custom fusion | flops 262144 | bytes 3145760 | tf_op jit(solution)/shard_map/while/body/scatter-add | solution.py:34
  125.8 3.0 gather_fusion.1
  132.7 3.4 %scatter_fusion = f32[256,32,128]{2,0,1:T(8,128)} fusion(f32[256,32,128]{2,0,1:T(8,128)} %get-tuple-element.258, s32[8]{0:T(128)S(1)} %get-tuple-element.237, f32[8,256,128]{2,1,0:T(8,128)S(1)} %copy.36), kind=kCustom, calls=%fused_computation.2.clone.1 | custom fusion | flops 262144 | bytes 3145760 | tf_op jit(solution)/shard_map/while/body/scatter-add | solution.py:34
  137.6 3.0 gather_fusion.1
  144.5 3.3 %scatter_fusion = f32[256,32,128]{2,0,1:T(8,128)} fusion(f32[256,32,128]{2,0,1:T(8,128)} %get-tuple-element.258, s32[8]{0:T(128)S(1)} %get-tuple-element.237, f32[8,256,128]{2,1,0:T(8,128)S(1)} %copy.36), kind=kCustom, calls=%fused_computation.2.clone.1 | custom fusion | flops 262144 | bytes 3145760 | tf_op jit(solution)/shard_map/while/body/scatter-add | solution.py:34
  149.4 3.0 gather_fusion.1
  156.3 3.4 %scatter_fusion = f32[256,32,128]{2,0,1:T(8,128)} fusion(f32[256,32,128]{2,0,1:T(8,128)} %get-tuple-element.258, s32[8]{0:T(128)S(1)} %get-tuple-element.237, f32[8,256,128]{2,1,0:T(8,128)S(1)} %copy.36), kind=kCustom, calls=%fused_computation.2.clone.1 | custom fusion | flops 262144 | bytes 3145760 | tf_op jit(solution)/shard_map/while/body/scatter-add | solution.py:34
  159.7 4.6 %copy_bitcast_fusion = f32[256,4096]{1,0:T(8,128)} fusion(f32[256,32,128]{2,0,1:T(8,128)} %get-tuple-element.122), kind=kLoop, calls=%fused_computation.31 | loop fusion | bytes 8388608 | tf_op jit(solution)/shard_map/reshape | solution.py:69
  164.4 125.5 %reduce-scatter.2.cloned.1.call-done = f32[16,4096]{1,0:T(8,128)} async-done(((f32[256,4096]{1,0:T(8,128)}), f32[16,4096]{1,0:T(8,128)}) %reduce-scatter.2.cloned.1.call-update) | async-done | bytes 262160 | tf_op jit(solution)/shard_map/reduce_scatter | solution.py:68
  290.9 6.8 %collective-permute-start = (bf16[16,4096]{1,0:T(8,128)(2,1)S(1)}, bf16[16,4096]{1,0:T(8,128)(2,1)S(1)}, u32[]{:S(2)}, u32[]{:S(2)}) collective-permute-start(bf16[16,4096]{1,0:T(8,128)(2,1)S(1)} %fusion.13), channel_id=1, source_target_pairs={{16,0},{32,16},{48,32},{64,48},{80,64},{96,80},{112,96},{128,112},... | collective-permute-start | bytes 393224 | tf_op jit(solution)/shard_map/ppermute | solution.py:10
  297.7 2.5 collective-permute-done
  (58 shorter events, 31.2 us)
Async XLA Ops:
  7.2 71.4 %all-gather.3.cloned.1.call-start = ((), (), s32[]{:S(2)}) async-start(), calls=%async_computation.2 | async-start | bytes 2228224 | tf_op jit(solution)/shard_map/all_gather | solution.py:52
  7.9 282.0 %reduce-scatter.2.cloned.1.call-start = ((), (), s32[]{:S(2)}) async-start(), calls=%async_computation.1 | async-start | bytes 4456448 | tf_op jit(solution)/shard_map/reduce_scatter | solution.py:68
  86.5 2.5 copy-start.1
  164.3 125.5 %copy-start = (bf16[1,16,4096]{2,1,0:T(8,128)(2,1)S(1)}, bf16[1,16,4096]{2,1,0:T(8,128)(2,1)}, u32[]{:S(2)}) copy-start(bf16[1,16,4096]{2,1,0:T(8,128)(2,1)} %param.10) | copy-start | bytes 393220
  290.9 9.3 %collective-permute-start = (bf16[16,4096]{1,0:T(8,128)(2,1)S(1)}, bf16[16,4096]{1,0:T(8,128)(2,1)S(1)}, u32[]{:S(2)}, u32[]{:S(2)}) collective-permute-start(bf16[16,4096]{1,0:T(8,128)(2,1)S(1)} %fusion.13), channel_id=1, source_target_pairs={{16,0},{32,16},{48,32},{64,48},{80,64},{96,80},{112,96},{128,112},... | collective-permute-start | bytes 393224 | tf_op jit(solution)/shard_map/ppermute | solution.py:10
Sparse Core Ops, SparseCore 0:
  11.3 67.2 all-gather.2
  164.5 125.3 reduce-scatter.1
where the time goes:
time: 309 us; the launch traced here: 308 us
  waiting for transfers between devices  197 us (64%)
  local copies, waits for them, and re-layouts  41.1 us (13%)
  other arithmetic  26.1 us (8%)
  matrix products  21.4 us (7%)
  between operations  14.7 us (5%)
  starting transfers between devices  6.9 us (2%)
    reduce_scatter x1, waiting for transfers between devices, shards(): lax.psum_scatter(partial_value.reshape(token_total, model_width), 'tensor...  126 us
    all_gather x1, waiting for transfers between devices, shards(): gathered = lax.all_gather(activations[0], 'tensor', axis=0, tiled=True)  68.4 us
    scatter-add x6, other arithmetic, advance(): partial_value = partial_value.at[:, model_block].add(backward)  20.2 us
    gather x6, local copies, waits for them, and re-layouts, advance(): act_part = jnp.take(act_blocks, model_block, axis=1)  18 us
    dot_general x6, matrix products, advance(): jnp.einsum('tsj,tsk->sjk', act_part, grad_part, preferred_element_type=jn...  13.5 us
    dot_general x6, matrix products, advance(): jnp.einsum('tsk,sjk->tsj', grad_part, tile_group, preferred_element_type=...  7.94 us
    ppermute x1, starting transfers between devices, passed_along(): return lax.ppermute(x, axis, pairs)  6.82 us
  transfers between devices with their start and end apart: 3, of which 3 were waited for; matrix products, arithmetic and copies ran while one was open for 0% of the time, Pallas kernels for 0%

commit v1 on v0

v1 whole, which is shorter than its diff:
```python
import functools

import jax
import jax.numpy as jnp
from jax import lax
from jax.experimental import pallas as pl
from jax.experimental.pallas import tpu as pltpu
from jax.sharding import PartitionSpec as P

BLK = 128
LEVELS = 32700.0
STEPS = 128.0
FLOOR = 2.0**-100


def branch_kernel(ids, h0, w0, h1, w1, out, acc):
    rows, width = h0.shape[0] * h0.shape[1], out.shape[-1] - BLK
    blocks = width // BLK
    slots = w0.shape[0]
    unroll = 4
    acc[...] = jnp.zeros_like(acc)
    for s, (h, w) in enumerate(((h0, w0), (h1, w1))):
        live_count = ids[s, slots]

        def some(t, _, s=s, h=h, w=w, live_count=live_count):
            found = []
            for u in range(unroll):
                j = t * unroll + u
                name = ids[s, j]
                live = j < live_count
                c = jnp.where(live, name // blocks, 0)
                b = jnp.where(live, name % blocks, blocks)
                left = h[:, :, pl.ds(pl.multiple_of(c * BLK, BLK), BLK)].reshape(rows, BLK)
                d = lax.dot_general(left, w[j], (((1,), (1,)), ((), ())), preferred_element_type=jnp.float32)
                found.append((b, d))
            for b, d in found:
                at = pl.ds(pl.multiple_of(b * BLK, BLK), BLK)
                acc[:, at] += d
            return 0

        lax.fori_loop(0, (live_count + unroll - 1) // unroll, some, 0)
    lane = lax.broadcasted_iota(jnp.int32, (rows, BLK), 1)

    def code(k, scales):
        at = pl.ds(pl.multiple_of(k * BLK, BLK), BLK)
        x = acc[:, at]
        top = jnp.maximum(jnp.max(jnp.abs(x), axis=1, keepdims=True), FLOOR)
        e = jnp.ceil(STEPS * jnp.log2(top))
        y = jnp.round(x * (LEVELS * jnp.exp2(e * (-1.0 / STEPS))))
        out[:, :, at] = y.astype(jnp.int32).astype(jnp.int16).reshape(out.shape[0], out.shape[1], BLK)
        return jnp.where(lane == k, e.astype(jnp.int32), scales)

    scales = lax.fori_loop(0, blocks, code, jnp.zeros((rows, BLK), jnp.int32))
    out[:, :, width:] = scales.astype(jnp.int16).reshape(out.shape[0], out.shape[1], BLK)


def total_kernel(parts, residual, out):
    count, rows, width = parts.shape[0], out.shape[0], out.shape[1]
    scales = [
        jnp.exp2(parts[i, :, width:].astype(jnp.int32).astype(jnp.float32) * (1.0 / STEPS)) * (1.0 / LEVELS)
        for i in range(count)
    ]
    for k in range(width // BLK):
        at = slice(k * BLK, (k + 1) * BLK)
        value = jnp.zeros((rows, BLK), jnp.float32)
        for i in range(count):
            value += parts[i, :, at].astype(jnp.int32).astype(jnp.float32) * scales[i][:, k : k + 1]
        out[:, at] = (residual[:, at].astype(jnp.float32) + value).astype(out.dtype)


def weight_kernel(ids, a0, a1, h0, h1, out):
    rows = a0.shape[0] * a0.shape[1]
    blocks = a0.shape[-1] // BLK
    slots = out.shape[0]
    unroll = 4
    live_count = ids[0, slots]

    def some(t, _):
        for u in range(unroll):
            j = t * unroll + u
            name = ids[0, j]
            live = j < live_count
            c = pl.ds(pl.multiple_of(jnp.where(live, name // blocks, 0) * BLK, BLK), BLK)
            b = pl.ds(pl.multiple_of(jnp.where(live, name % blocks, 0) * BLK, BLK), BLK)
            act = jnp.concatenate([a0[:, :, b].reshape(rows, BLK), a1[:, :, b].reshape(rows, BLK)], axis=0)
            hid = jnp.concatenate([h0[:, :, c].reshape(rows, BLK), h1[:, :, c].reshape(rows, BLK)], axis=0)
            d = lax.dot_general(act, hid, (((0,), (0,)), ((), ())), preferred_element_type=jnp.float32)
            out[j] = jnp.where(live, d, 0.0).astype(out.dtype)
        return 0

    trips = (live_count + unroll - 1) // unroll
    lax.fori_loop(0, trips, some, 0)

    def clear(j, _):
        out[j] = jnp.zeros((BLK, BLK), out.dtype)
        return 0

    lax.fori_loop(trips * unroll, slots, clear, 0)


SMEM = pl.BlockSpec(memory_space=pltpu.SMEM)
VMEM = pl.BlockSpec(memory_space=pltpu.VMEM)


def shards(activations, hidden_grad, residual_grad, weight_tiles, tile_ids, tile_counts):
    count = lax.axis_size("tensor")
    chips = count // 2
    rows, width = activations.shape[1:]
    slots = weight_tiles.shape[2]
    core = lax.axis_index("tensor") % 2
    swap = [(i, i ^ 1) for i in range(count)]
    same_core = [[2 * i + c for i in range(chips)] for c in range(2)]

    tiles = weight_tiles[0, 0]
    tiles_other = lax.ppermute(tiles, "tensor", swap)
    names = jnp.concatenate([tile_ids[0, 0], tile_counts[0], jnp.zeros((7,), jnp.int32)])
    names_other = lax.ppermute(names, "tensor", swap)
    hidden = hidden_grad[0].reshape(chips, 2, rows, -1)
    hidden_here = lax.dynamic_index_in_dim(hidden, core, 1, keepdims=False)
    hidden_there = lax.dynamic_index_in_dim(hidden, 1 - core, 1, keepdims=False)
    hidden_other = lax.ppermute(hidden_there, "tensor", swap)
    acts = lax.all_to_all(
        jnp.broadcast_to(activations, (chips, rows, width)), "tensor", 0, 0, axis_index_groups=same_core, tiled=True
    )
    acts_other = lax.ppermute(acts, "tensor", swap)
    both_names = jnp.stack([names, names_other])

    sent = pl.pallas_call(
        branch_kernel,
        out_shape=jax.ShapeDtypeStruct((chips, rows, width + BLK), jnp.int16),
        in_specs=[SMEM, VMEM, VMEM, VMEM, VMEM],
        out_specs=VMEM,
        scratch_shapes=[pltpu.VMEM((chips * rows, width + BLK), jnp.float32)],
        compiler_params=pltpu.CompilerParams(vmem_limit_bytes=40 << 20),
        cost_estimate=pl.CostEstimate(flops=4 << 30, bytes_accessed=6 << 20, transcendentals=0),
        name="branch",
    )(both_names, hidden_here, tiles, hidden_other, tiles_other)
    parts = lax.all_to_all(sent, "tensor", 0, 0, axis_index_groups=same_core, tiled=True)
    grads = pl.pallas_call(
        weight_kernel,
        out_shape=jax.ShapeDtypeStruct(tiles.shape, jnp.bfloat16),
        in_specs=[SMEM, VMEM, VMEM, VMEM, VMEM],
        out_specs=VMEM,
        compiler_params=pltpu.CompilerParams(vmem_limit_bytes=40 << 20),
        cost_estimate=pl.CostEstimate(flops=4 << 30, bytes_accessed=6 << 20, transcendentals=0),
        name="weight_grads",
    )(names[None], acts, acts_other, hidden_here, hidden_there)
    total = pl.pallas_call(
        total_kernel,
        out_shape=jax.ShapeDtypeStruct((rows, width), jnp.bfloat16),
        in_specs=[VMEM, VMEM],
        out_specs=VMEM,
        compiler_params=pltpu.CompilerParams(vmem_limit_bytes=40 << 20),
        name="total",
    )(parts, residual_grad[0])
    pipes = lax.axis_size("pipe")
    received = lax.ppermute(total, "pipe", [(i, i - 1) for i in range(1, pipes)])
    return received[None], grads[None, None]


def solution(mesh):
    return jax.shard_map(
        shards,
        mesh=mesh,
        in_specs=(
            P("pipe", "tensor", None),
            P("pipe", None, "tensor"),
            P("pipe", "tensor", None),
            P("pipe", "tensor", None, None, None),
            P("pipe", "tensor", None),
            P("pipe", "tensor"),
        ),
        out_specs=(P("pipe", "tensor", None), P("pipe", "tensor", None, None, None)),
        check_vma=False,
    )
```

time: 309 us -> 83.7 us (0.27)
  waiting for transfers between devices: 197 us -> 12.2 us
  local copies, waits for them, and re-layouts: 41.1 us -> 4.29 us
  other arithmetic: 26.1 us -> 0.16 us
  blocking collectives: 0 us -> 24.9 us
  matrix products: 21.4 us -> 0 us
  starting transfers between devices: 6.9 us -> 25.7 us
  Pallas kernels: 0 us -> 14.7 us
  between operations: 14.7 us -> 1.41 us
    reduce_scatter x1 -> x0, waiting for transfers between devices: 126 us -> none  [shards(): lax.psum_scatter(partial_value.reshape(token_total, model_width), 'tensor...]
    all_gather x1 -> x0, waiting for transfers between devices: 68.4 us -> none  [shards(): gathered = lax.all_gather(activations[0], 'tensor', axis=0, tiled=True)]
    all_to_all x0 -> x1, blocking collectives: none -> 24.9 us  [shards(): lax.all_to_all(sent, 'tensor', 0, 0, axis_index_groups=same_core, tiled=T...]
    gather x12 -> x0, local copies, waits for them, and re-layouts: 21.9 us -> none  [the longest x6 18 us: advance(): act_part = jnp.take(act_blocks, model_block, axis=1)]
    dot_general x12 -> x0, matrix products: 21.4 us -> none  [the longest x6 13.5 us: advance(): jnp.einsum('tsj,tsk->sjk', act_part, grad_part, preferred_element_type=jn...]
    scatter-add x6 -> x0, other arithmetic: 20.2 us -> none  [advance(): partial_value = partial_value.at[:, model_block].add(backward)]
    pallas_call x0 -> x3, Pallas kernels: none -> 14.7 us  [the longest x1 9.08 us: shards(): pl.pallas_call(branch_kernel, out_shape=jax.ShapeDtypeStruct((chips, rows...]
    ppermute x1 -> x5, starting transfers between devices: 6.82 us -> 19.6 us  [the longest x1 11.3 us: shards(): lax.ppermute(total, 'pipe', [(i, i - 1) for i in range(1, pipes)])]
  transfers between devices with their start and end apart: 3 -> 6, of which waited for: 3 -> 2; matrix products, arithmetic and copies ran while one was open for 0% -> 3% of each run, Pallas kernels for 0% -> 18%
where the time goes in v1:
time: 83.7 us; the launch traced here: 83.3 us
  starting transfers between devices  25.7 us (31%)
  blocking collectives  24.9 us (30%)
  Pallas kernels  14.7 us (18%)
  waiting for transfers between devices  12.2 us (15%)
  local copies, waits for them, and re-layouts  4.29 us (5%)
  between operations  1.41 us (2%)
    all_to_all x1, blocking collectives, shards(): lax.all_to_all(sent, 'tensor', 0, 0, axis_index_groups=same_core, tiled=T...  24.9 us
    all_to_all x1, waiting for transfers between devices, shards(): lax.all_to_all(jnp.broadcast_to(activations, (chips, rows, width)), 'tens...  11.4 us
    ppermute x1, starting transfers between devices, shards(): lax.ppermute(total, 'pipe', [(i, i - 1) for i in range(1, pipes)])  11.3 us
    pallas_call x1, Pallas kernels, shards(): pl.pallas_call(branch_kernel, out_shape=jax.ShapeDtypeStruct((chips, rows...  9.08 us
    all_to_all x1, starting transfers between devices, shards(): lax.all_to_all(jnp.broadcast_to(activations, (chips, rows, width)), 'tens...  6.03 us
    pallas_call x1, Pallas kernels, shards(): pl.pallas_call(weight_kernel, out_shape=jax.ShapeDtypeStruct(tiles.shape,...  4.98 us
    unnamed x9, local copies, waits for them, and re-layouts  2.26 us
    ppermute x1, starting transfers between devices, shards(): names_other = lax.ppermute(names, 'tensor', swap)  2.19 us
  transfers between devices with their start and end apart: 6, of which 2 were waited for; matrix products, arithmetic and copies ran while one was open for 3% of the time, Pallas kernels for 18%

profile of v1, /device:TPU:8, one launch (start us, length us, event | category | flops | bytes accessed | tf_op | source)
XLA Modules:
  0.0 83.3 jit_solution(599245039876283202)
XLA Ops:
  0.6 0.0 copy-start.2
  0.6 2.1 %collective-permute-start.2 = (bf16[64,128,128]{2,1,0:T(8,128)(2,1)}, bf16[64,128,128]{2,1,0:T(8,128)(2,1)}, u32[]{:S(2)}, u32[]{:S(2)}) collective-permute-start(bf16[64,128,128]{2,1,0:T(8,128)(2,1)} %bitcast.22), channel_id=1, source_target_pairs={{0,1},{1,0},{2,3},{3,2},{4,5},{5,4},{6,7},{7,6},{8,9},{9,8},{10,11... | collective-permute-start | bytes 6291464 | tf_op jit(solution)/shard_map/ppermute | solution.py:115
  2.7 2.0 %broadcast_in_dim.16 = bf16[8,16,4096]{2,1,0:T(8,128)(2,1)} broadcast(bf16[16,4096]{1,0:T(8,128)(2,1)} %bitcast.25), dimensions={1,2} | broadcast | bytes 1179648 | tf_op jit(solution)/shard_map/broadcast_in_dim | solution.py:123
  4.7 6.0 %all-to-all-start.1 = ((bf16[8,16,4096]{2,1,0:T(8,128)(2,1)}), bf16[8,16,4096]{2,1,0:T(8,128)(2,1)S(1)}, u32[]{:S(2)}, u32[]{:S(2)}) async-start(bf16[8,16,4096]{2,1,0:T(8,128)(2,1)} %broadcast_in_dim.16), calls=%async_computation.1 | async-start | bytes 2097152 | tf_op jit(solution)/shard_map/all_to_all | solution.py:122
  10.8 2.1 %collective-permute-start.1 = (bf16[8,16,896]{2,1,0:T(8,128)(2,1)S(1)}, bf16[8,16,896]{2,1,0:T(8,128)(2,1)S(1)}, u32[]{:S(2)}, u32[]{:S(2)}) collective-permute-start(bf16[8,16,896]{2,1,0:T(8,128)(2,1)S(1)} %get-tuple-element.2.h1), channel_id=1, source_target_pairs={{0,1},{1,0},{2,3},{3,2},{4,5},{5,4},{6,7},{7,6},{8,9},{9,8},{10,11... | collective-permute-start | bytes 688136 | tf_op jit(solution)/shard_map/ppermute | solution.py:121
  13.6 0.1 pad_add_fusion.1
  13.7 2.2 %collective-permute-start = (s32[72]{0:T(128)S(1)}, s32[72]{0:T(128)S(1)}, u32[]{:S(2)}, u32[]{:S(2)}) collective-permute-start(s32[72]{0:T(128)S(1)} %pad_add_fusion.1), channel_id=1, source_target_pairs={{0,1},{1,0},{2,3},{3,2},{4,5},{5,4},{6,7},{7,6},{8,9},{9,8},{10,11... | collective-permute-start | bytes 872 | tf_op jit(solution)/shard_map/ppermute | solution.py:117
  15.9 0.1 fusion.ids
  15.9 0.7 collective-permute-done
  16.7 11.4 %all-to-all-done.1.a0 = bf16[8,16,4096]{2,1,0:T(8,128)(2,1)S(1)} async-done(((bf16[8,16,4096]{2,1,0:T(8,128)(2,1)}), bf16[8,16,4096]{2,1,0:T(8,128)(2,1)S(1)}, u32[]{:S(2)}, u32[]{:S(2)}) %all-to-all-start.1) | async-done | bytes 1048608 | tf_op jit(solution)/shard_map/all_to_all | solution.py:122
  28.1 1.9 %collective-permute-start.4 = (bf16[8,16,4096]{2,1,0:T(8,128)(2,1)S(1)}, bf16[8,16,4096]{2,1,0:T(8,128)(2,1)S(1)}, u32[]{:S(2)}, u32[]{:S(2)}) collective-permute-start(bf16[8,16,4096]{2,1,0:T(8,128)(2,1)S(1)} %all-to-all-done.1.a0), channel_id=1, source_target_pairs={{0,1},{1,0},{2,3},{3,2},{4,5},{5,4},{6,7},{7,6},{8,9},{9,8},{10,11... | collective-permute-start | bytes 3145736 | tf_op jit(solution)/shard_map/ppermute | solution.py:125
  30.0 0.0 collective-permute-done.1.h1
  30.1 0.0 collective-permute-done.2.w1
  30.1 0.0 copy-start.1
  30.1 1.6 %copy-done.1 = bf16[1,1,64,128,128]{4,3,2,1,0:T(8,128)(2,1)S(1)} copy-done((bf16[1,1,64,128,128]{4,3,2,1,0:T(8,128)(2,1)S(1)}, bf16[1,1,64,128,128]{4,3,2,1,0:T(8,128)(2,1)}, u32[]{:S(2)}) %copy-start.1) | copy-done | bytes 2097176
  31.7 9.1 %branch.1 = s16[8,16,4224]{2,1,0:T(8,128)(2,1)S(1)} custom-call(s32[2,72]{1,0:T(2,128)S(1)} %pad_add_fusion.ids, bf16[8,16,896]{2,1,0:T(8,128)(2,1)S(1)} %get-tuple-element.3.h0, bf16[64,128,128]{2,1,0:T(8,128)(2,1)S(1)} %bitcast.23, bf16[8,16,896]{2,1,0:T(8,128)(2,1)S(1)} %collective-permute-done.1.h1, bf16[64,128,128]{2,1,0:T(8,128)(2,1)} %collective-permute-done.2.w1), custom_call_target="tpu_custom_call" | custom-call | flops 4294967296 | bytes 6291456 | tf_op jit(solution)/shard_map/branch/pallas_call | solution.py:128
  40.7 0.0 copy-start
  40.8 24.9 %all_to_all.10.parts = s16[8,16,4224]{2,1,0:T(8,128)(2,1)S(1)} all-to-all(s16[8,16,4224]{2,1,0:T(8,128)(2,1)S(1)} %branch.1), channel_id=1, replica_groups={{0,2,4,6,8,10,12,14},{1,3,5,7,9,11,13,15},{16,18,20,22,24,26,28,30},{17..., dimensions={0} | all-to-all | bytes 2162688 | tf_op jit(solution)/shard_map/all_to_all | solution.py:138
  65.6 0.7 total.1
  66.3 11.3 %collective-permute-start.3 = (bf16[16,4096]{1,0:T(8,128)(2,1)S(1)}, bf16[16,4096]{1,0:T(8,128)(2,1)S(1)}, u32[]{:S(2)}, u32[]{:S(2)}) collective-permute-start(bf16[16,4096]{1,0:T(8,128)(2,1)S(1)} %total.1), channel_id=1, source_target_pairs={{16,0},{32,16},{48,32},{64,48},{80,64},{96,80},{112,96},{128,112},... | collective-permute-start | bytes 393224 | tf_op jit(solution)/shard_map/ppermute | solution.py:157
  77.6 0.0 collective-permute-done.4.a1
  77.7 5.0 %weight_grads.1 = bf16[64,128,128]{2,1,0:T(8,128)(2,1)} custom-call(s32[1,72]{1,0:T(1,128)S(1)} %fusion.ids, bf16[8,16,4096]{2,1,0:T(8,128)(2,1)S(1)} %all-to-all-done.1.a0, bf16[8,16,4096]{2,1,0:T(8,128)(2,1)S(1)} %collective-permute-done.4.a1, bf16[8,16,896]{2,1,0:T(8,128)(2,1)S(1)} %get-tuple-element.3.h0, bf16[8,16,896]{2,1,0:T(8,128)(2,1)S(1)} %get-tuple-element.2.h1), custom_call_target="tpu_custom_call" | custom-call | flops 4294967296 | bytes 6291456 | tf_op jit(solution)/shard_map/weight_grads/pallas_call | solution.py:139
  82.6 0.0 collective-permute-done.3
  82.6 0.7 copy.14
  (7 shorter events, 0.1 us)
Async XLA Ops:
  0.6 10.1 %copy-start.2 = (bf16[1,256,896]{2,1,0:T(8,128)(2,1)S(1)}, bf16[1,256,896]{2,1,0:T(8,128)(2,1)}, u32[]{:S(2)}) copy-start(bf16[1,256,896]{2,1,0:T(8,128)(2,1)} %param.7) | copy-start | bytes 1376260
  0.6 29.4 %collective-permute-start.2 = (bf16[64,128,128]{2,1,0:T(8,128)(2,1)}, bf16[64,128,128]{2,1,0:T(8,128)(2,1)}, u32[]{:S(2)}, u32[]{:S(2)}) collective-permute-start(bf16[64,128,128]{2,1,0:T(8,128)(2,1)} %bitcast.22), channel_id=1, source_target_pairs={{0,1},{1,0},{2,3},{3,2},{4,5},{5,4},{6,7},{7,6},{8,9},{9,8},{10,11... | collective-permute-start | bytes 6291464 | tf_op jit(solution)/shard_map/ppermute | solution.py:115
  2.7 10.9 %copy-start.3 = (s32[1,1,64]{2,1,0:T(1,128)S(1)}, s32[1,1,64]{2,1,0:T(1,128)}, u32[]{:S(2)}) copy-start(s32[1,1,64]{2,1,0:T(1,128)} %param.10) | copy-start | bytes 772
  4.7 23.4 %all-to-all-start.1 = ((bf16[8,16,4096]{2,1,0:T(8,128)(2,1)}), bf16[8,16,4096]{2,1,0:T(8,128)(2,1)S(1)}, u32[]{:S(2)}, u32[]{:S(2)}) async-start(bf16[8,16,4096]{2,1,0:T(8,128)(2,1)} %broadcast_in_dim.16), calls=%async_computation.1 | async-start | bytes 2097152 | tf_op jit(solution)/shard_map/all_to_all | solution.py:122
  10.8 19.3 %collective-permute-start.1 = (bf16[8,16,896]{2,1,0:T(8,128)(2,1)S(1)}, bf16[8,16,896]{2,1,0:T(8,128)(2,1)S(1)}, u32[]{:S(2)}, u32[]{:S(2)}) collective-permute-start(bf16[8,16,896]{2,1,0:T(8,128)(2,1)S(1)} %get-tuple-element.2.h1), channel_id=1, source_target_pairs={{0,1},{1,0},{2,3},{3,2},{4,5},{5,4},{6,7},{7,6},{8,9},{9,8},{10,11... | collective-permute-start | bytes 688136 | tf_op jit(solution)/shard_map/ppermute | solution.py:121
  13.7 3.0 %collective-permute-start = (s32[72]{0:T(128)S(1)}, s32[72]{0:T(128)S(1)}, u32[]{:S(2)}, u32[]{:S(2)}) collective-permute-start(s32[72]{0:T(128)S(1)} %pad_add_fusion.1), channel_id=1, source_target_pairs={{0,1},{1,0},{2,3},{3,2},{4,5},{5,4},{6,7},{7,6},{8,9},{9,8},{10,11... | collective-permute-start | bytes 872 | tf_op jit(solution)/shard_map/ppermute | solution.py:117
  28.1 49.5 %collective-permute-start.4 = (bf16[8,16,4096]{2,1,0:T(8,128)(2,1)S(1)}, bf16[8,16,4096]{2,1,0:T(8,128)(2,1)S(1)}, u32[]{:S(2)}, u32[]{:S(2)}) collective-permute-start(bf16[8,16,4096]{2,1,0:T(8,128)(2,1)S(1)} %all-to-all-done.1.a0), channel_id=1, source_target_pairs={{0,1},{1,0},{2,3},{3,2},{4,5},{5,4},{6,7},{7,6},{8,9},{9,8},{10,11... | collective-permute-start | bytes 3145736 | tf_op jit(solution)/shard_map/ppermute | solution.py:125
  30.1 1.6 %copy-start.1 = (bf16[1,1,64,128,128]{4,3,2,1,0:T(8,128)(2,1)S(1)}, bf16[1,1,64,128,128]{4,3,2,1,0:T(8,128)(2,1)}, u32[]{:S(2)}) copy-start(bf16[1,1,64,128,128]{4,3,2,1,0:T(8,128)(2,1)} %param.9) | copy-start | bytes 6291460
  40.7 24.9 %copy-start = (bf16[1,16,4096]{2,1,0:T(8,128)(2,1)S(1)}, bf16[1,16,4096]{2,1,0:T(8,128)(2,1)}, u32[]{:S(2)}) copy-start(bf16[1,16,4096]{2,1,0:T(8,128)(2,1)} %param.8) | copy-start | bytes 393220
  66.3 16.3 %collective-permute-start.3 = (bf16[16,4096]{1,0:T(8,128)(2,1)S(1)}, bf16[16,4096]{1,0:T(8,128)(2,1)S(1)}, u32[]{:S(2)}, u32[]{:S(2)}) collective-permute-start(bf16[16,4096]{1,0:T(8,128)(2,1)S(1)} %total.1), channel_id=1, source_target_pairs={{16,0},{32,16},{48,32},{64,48},{80,64},{96,80},{112,96},{128,112},... | collective-permute-start | bytes 393224 | tf_op jit(solution)/shard_map/ppermute | solution.py:157

commit v2 on v1

v2 whole, which is shorter than its diff:
```python
import jax
import jax.numpy as jnp
from jax import lax
from jax.experimental import pallas as pl
from jax.experimental.pallas import tpu as pltpu
from jax.sharding import PartitionSpec as P

BLK = 128
LEVELS = 32700.0
STEPS = 128.0
FLOOR = 2.0**-100
GROUP = 16
PIECES = 2


def spread_kernel(acts, out, held, sems):
    fetch = pltpu.make_async_copy(acts.at[0], held, sems.at[0])
    fetch.start()
    fetch.wait()
    copies = [pltpu.make_async_copy(held, out.at[i], sems.at[i]) for i in range(out.shape[0])]
    for copy in copies:
        copy.start()
    for copy in copies:
        copy.wait()


def hidden_copies(hidden, held, sems):
    core = lax.axis_index("tensor") % 2
    width = hidden.shape[-1]
    return [
        pltpu.make_async_copy(hidden.at[:, which], held.at[i, :, :, pl.ds(0, width)], sems.at[i])
        for i, which in enumerate((core, 1 - core))
    ]


def encode(read, write, write_scale, blocks, rows):
    top = jnp.full((rows, BLK), FLOOR, jnp.float32)
    for k in range(blocks):
        top = jnp.maximum(top, jnp.abs(read(k)))
    e = jnp.ceil(STEPS * jnp.log2(top))
    write_scale(e.astype(jnp.int32).astype(jnp.int16))
    scale = LEVELS * jnp.exp2(e * (-1.0 / STEPS))
    for k in range(blocks):
        write(k, jnp.round(read(k) * scale).astype(jnp.int32).astype(jnp.int16))


def decode_scale(coded):
    return jnp.exp2(coded.astype(jnp.int32).astype(jnp.float32) * (1.0 / STEPS)) * (1.0 / LEVELS)


def encode_rows(source, i, out):
    rows, width = out.shape[1], out.shape[2] - BLK

    def write(k, value):
        out[i, :, k * BLK : (k + 1) * BLK] = value

    def write_scale(value):
        out[i, :, width:] = value

    encode(lambda k: source(k * BLK, (k + 1) * BLK), write, write_scale, width // BLK, rows)


def branch_kernel(ids, counts, hidden, tiles, keep, *refs):
    codes, (give, held, w, sems) = refs[:-4], refs[-4:]
    share = codes[0].shape[0]
    chips, rows, width = keep.shape
    blocks = width // BLK
    slots = w.shape[0]
    empty = hidden.shape[-1] // BLK
    live_count = counts[0, 0]
    parts = slots // GROUP
    tile_copies = [
        pltpu.make_async_copy(tiles.at[pl.ds(g * GROUP, GROUP)], w.at[pl.ds(g * GROUP, GROUP)], sems.at[2 + g])
        for g in range(parts)
    ]
    copies = hidden_copies(hidden, held, sems)
    for copy in copies + tile_copies:
        copy.start()
    held[:, :, :, empty * BLK :] = jnp.zeros((2, chips, rows, BLK), jnp.bfloat16)
    keep[...] = jnp.zeros_like(keep)
    give[...] = jnp.zeros_like(give)
    for copy in copies:
        copy.wait()
    for g in range(parts):
        tile_copies[g].wait()

        @pl.when(g * GROUP < live_count)
        def _(g=g):
            found = []
            for j in range(g * GROUP, (g + 1) * GROUP):
                name = ids[0, j]
                live = j < live_count
                c = jnp.where(live, name // blocks, empty)
                b = jnp.where(live, name % blocks, 0)
                left = held[:, :, :, pl.ds(pl.multiple_of(c * BLK, BLK), BLK)].reshape(2 * chips * rows, BLK)
                d = lax.dot_general(left, w[j], (((1,), (1,)), ((), ())), preferred_element_type=jnp.float32)
                found.append((b, d))
            for b, d in found:
                at = pl.ds(pl.multiple_of(b * BLK, BLK), BLK)
                keep[:, :, at] += d[: chips * rows].reshape(chips, rows, BLK)
                give[:, :, at] += d[chips * rows :].reshape(chips, rows, BLK)

    for i in range(chips):
        encode_rows(lambda lo, hi, i=i: give[i, :, lo:hi], i % share, codes[i // share])


def merge_kernel(keep, *refs):
    gots, (out, both) = refs[:-2], refs[-2:]
    chips, rows, width = keep.shape
    share = gots[0].shape[0]
    for i in range(chips):
        got, g = gots[i // share], i % share
        scale = decode_scale(got[g, :, width:])
        for k in range(width // BLK):
            at = slice(k * BLK, (k + 1) * BLK)
            both[i, :, at] = keep[i, :, at] + got[g, :, at].astype(jnp.int32).astype(jnp.float32) * scale
        encode_rows(lambda lo, hi, i=i: both[i, :, lo:hi], i, out)


def total_kernel(parts, residual, out):
    count, rows, width = parts.shape[0], out.shape[1], out.shape[2]
    scales = [decode_scale(parts[i, :, width:]) for i in range(count)]
    for k in range(width // BLK):
        at = slice(k * BLK, (k + 1) * BLK)
        value = jnp.zeros((rows, BLK), jnp.float32)
        for i in range(count):
            value += parts[i, :, at].astype(jnp.int32).astype(jnp.float32) * scales[i]
        out[0, :, at] = (residual[:, at].astype(jnp.float32) + value).astype(out.dtype)


def weight_kernel(ids, counts, a0, a1, hidden, out, held, sems):
    chips, rows = a0.shape[:2]
    blocks = a0.shape[-1] // BLK
    slots = out.shape[0]
    live_count = counts[0, 0]
    copies = hidden_copies(hidden, held, sems)
    for copy in copies:
        copy.start()
    for copy in copies:
        copy.wait()

    def some(t, _):
        for u in range(GROUP):
            j = t * GROUP + u
            name = ids[0, j]
            live = j < live_count
            c = pl.ds(pl.multiple_of(jnp.where(live, name // blocks, 0) * BLK, BLK), BLK)
            b = pl.ds(pl.multiple_of(jnp.where(live, name % blocks, 0) * BLK, BLK), BLK)
            act = jnp.concatenate([a[:, :, b].reshape(chips * rows, BLK) for a in (a0, a1)], axis=0)
            hid = held[:, :, :, c].reshape(2 * chips * rows, BLK)
            d = lax.dot_general(act, hid, (((0,), (0,)), ((), ())), preferred_element_type=jnp.float32)
            out[j] = jnp.where(live, d, 0.0).astype(out.dtype)
        return 0

    trips = (live_count + GROUP - 1) // GROUP
    lax.fori_loop(0, trips, some, 0)

    def clear(j, _):
        out[j] = jnp.zeros((BLK, BLK), out.dtype)
        return 0

    lax.fori_loop(trips * GROUP, slots, clear, 0)


SMEM = pl.BlockSpec(memory_space=pltpu.SMEM)
VMEM = pl.BlockSpec(memory_space=pltpu.VMEM)
ANY = pl.BlockSpec(memory_space=pl.ANY)
PARAMS = pltpu.CompilerParams(vmem_limit_bytes=16 << 20)


def shards(activations, hidden_grad, residual_grad, weight_tiles, tile_ids, tile_counts):
    count = lax.axis_size("tensor")
    chips = count // 2
    rows, width = activations.shape[1:]
    slots = weight_tiles.shape[2]
    hidden_width = hidden_grad.shape[2]
    swap = [(i, i ^ 1) for i in range(count)]
    same_core = [[2 * i + c for i in range(chips)] for c in range(2)]
    in_hbm = lambda x: pltpu.with_memory_space_constraint(x, pltpu.HBM)

    acts_copies = pl.pallas_call(
        spread_kernel,
        out_shape=jax.ShapeDtypeStruct((chips, rows, width), jnp.bfloat16),
        in_specs=[ANY],
        out_specs=ANY,
        scratch_shapes=[pltpu.VMEM((rows, width), jnp.bfloat16), pltpu.SemaphoreType.DMA((chips,))],
        compiler_params=PARAMS,
        name="spread",
    )(in_hbm(activations))

    tiles, hidden, acts_copies = lax.optimization_barrier((weight_tiles[0, 0], hidden_grad[0], acts_copies))
    acts = lax.all_to_all(acts_copies, "tensor", 0, 0, axis_index_groups=same_core, tiled=True)
    tiles = in_hbm(tiles)
    hidden = in_hbm(hidden.reshape(chips, 2, rows, hidden_width))
    coded = jax.ShapeDtypeStruct((chips, rows, width + BLK), jnp.int16)
    partial = pltpu.VMEM((chips, rows, width), jnp.float32)
    share = jax.ShapeDtypeStruct((chips // PIECES, rows, width + BLK), jnp.int16)
    keep, *gives = pl.pallas_call(
        branch_kernel,
        out_shape=(jax.ShapeDtypeStruct((chips, rows, width), jnp.float32),) + (share,) * PIECES,
        in_specs=[SMEM, SMEM, ANY, ANY],
        out_specs=(VMEM,) * (1 + PIECES),
        scratch_shapes=[
            partial,
            pltpu.VMEM((2, chips, rows, hidden_width + BLK), jnp.bfloat16),
            pltpu.VMEM((slots, BLK, BLK), jnp.bfloat16),
            pltpu.SemaphoreType.DMA((2 + slots // GROUP,)),
        ],
        compiler_params=PARAMS,
        cost_estimate=pl.CostEstimate(flops=1 << 10, bytes_accessed=1 << 10, transcendentals=0),
        name="branch",
    )(tile_ids[0], tile_counts, hidden, tiles)
    gots = [lax.ppermute(give, "tensor", swap) for give in gives]
    sent = pl.pallas_call(
        merge_kernel,
        out_shape=coded,
        in_specs=[VMEM] * (1 + PIECES),
        out_specs=VMEM,
        scratch_shapes=[partial],
        compiler_params=PARAMS,
        cost_estimate=pl.CostEstimate(flops=1 << 10, bytes_accessed=1 << 10, transcendentals=0),
        name="merge",
    )(keep, *gots)
    parts = lax.all_to_all(sent, "tensor", 0, 0, axis_index_groups=same_core, tiled=True)
    acts, _ = lax.optimization_barrier((acts, sent))
    acts_other = lax.ppermute(acts, "tensor", swap)
    grads = pl.pallas_call(
        weight_kernel,
        out_shape=jax.ShapeDtypeStruct((slots, BLK, BLK), jnp.bfloat16),
        in_specs=[SMEM, SMEM, VMEM, VMEM, ANY],
        out_specs=VMEM,
        scratch_shapes=[
            pltpu.VMEM((2, chips, rows, hidden_width), jnp.bfloat16),
            pltpu.SemaphoreType.DMA((2,)),
        ],
        compiler_params=PARAMS,
        cost_estimate=pl.CostEstimate(flops=1 << 10, bytes_accessed=1 << 10, transcendentals=0),
        name="weight_grads",
    )(tile_ids[0], tile_counts, acts, acts_other, hidden)
    parts, grads = lax.optimization_barrier((parts, grads))
    total = pl.pallas_call(
        total_kernel,
        out_shape=jax.ShapeDtypeStruct((1, rows, width), jnp.bfloat16),
        in_specs=[VMEM, VMEM],
        out_specs=VMEM,
        compiler_params=PARAMS,
        name="total",
    )(parts, residual_grad[0])
    pipes = lax.axis_size("pipe")
    received = lax.ppermute(total, "pipe", [(i, i - 1) for i in range(1, pipes)])
    return received, grads[None, None]


def solution(mesh):
    return jax.shard_map(
        shards,
        mesh=mesh,
        in_specs=(
            P("pipe", "tensor", None),
            P("pipe", None, "tensor"),
            P("pipe", "tensor", None),
            P("pipe", "tensor", None, None, None),
            P("pipe", "tensor", None),
            P("pipe", "tensor"),
        ),
        out_specs=(P("pipe", "tensor", None), P("pipe", "tensor", None, None, None)),
        check_vma=False,
    )
```

time: 83.7 us -> 64.2 us (0.77)
  blocking collectives: 24.9 us -> 0 us
  waiting for transfers between devices: 12.2 us -> 19.7 us
  local copies, waits for them, and re-layouts: 4.29 us -> 0.66 us
  starting transfers between devices: 25.7 us -> 29.2 us
  Pallas kernels: 14.7 us -> 12.9 us
    all_to_all x1 -> x0, blocking collectives: 24.9 us -> none  [shards(): lax.all_to_all(sent, 'tensor', 0, 0, axis_index_groups=same_core, tiled=T...]
    all_to_all x1 -> x2, starting transfers between devices: 6.03 us -> 10.8 us  [the longest x1 6.04 us: shards(): lax.all_to_all(acts_copies, 'tensor', 0, 0, axis_index_groups=same_core,...]
    all_to_all x1 -> x2, waiting for transfers between devices: 11.4 us -> 15.6 us  [the longest x1 12.3 us: shards(): lax.all_to_all(sent, 'tensor', 0, 0, axis_index_groups=same_core, tiled=T...]
    ppermute x1, waiting for transfers between devices: 0.01 us -> 2.5 us  [shards(): lax.ppermute(total, 'pipe', [(i, i - 1) for i in range(1, pipes)])]
    ppermute x3 -> x2, starting transfers between devices: 6.37 us -> 4.33 us  [shards(): gots = [lax.ppermute(give, 'tensor', swap) for give in gives]]
    broadcast_in_dim x1 -> x0, local copies, waits for them, and re-layouts: 1.98 us -> none  [shards(): jnp.broadcast_to(activations, (chips, rows, width))]
    pallas_call x3 -> x5, Pallas kernels: 14.7 us -> 12.9 us  [the longest x1 4.64 us: shards(): pl.pallas_call(weight_kernel, out_shape=jax.ShapeDtypeStruct((slots, BLK,...]
    unnamed x9 -> x5, local copies, waits for them, and re-layouts: 2.26 us -> 0.66 us
  transfers between devices with their start and end apart: 6 -> 6, of which waited for: 2 -> 4; matrix products, arithmetic and copies ran while one was open for 3% -> 0% of each run, Pallas kernels for 18% -> 17%
where the time goes in v2:
time: 64.2 us; the launch traced here: 63.8 us
  starting transfers between devices  29.2 us (45%)
  waiting for transfers between devices  19.7 us (31%)
  Pallas kernels  12.9 us (20%)
  between operations  1.38 us (2%)
  local copies, waits for them, and re-layouts  0.66 us (1%)
    all_to_all x1, waiting for transfers between devices, shards(): lax.all_to_all(sent, 'tensor', 0, 0, axis_index_groups=same_core, tiled=T...  12.3 us
    ppermute x1, starting transfers between devices, shards(): lax.ppermute(total, 'pipe', [(i, i - 1) for i in range(1, pipes)])  12.2 us
    all_to_all x1, starting transfers between devices, shards(): lax.all_to_all(acts_copies, 'tensor', 0, 0, axis_index_groups=same_core,...  6.04 us
    all_to_all x1, starting transfers between devices, shards(): lax.all_to_all(sent, 'tensor', 0, 0, axis_index_groups=same_core, tiled=T...  4.74 us
    pallas_call x1, Pallas kernels, shards(): pl.pallas_call(weight_kernel, out_shape=jax.ShapeDtypeStruct((slots, BLK,...  4.64 us
    ppermute x2, starting transfers between devices, shards(): gots = [lax.ppermute(give, 'tensor', swap) for give in gives]  4.33 us
    pallas_call x1, Pallas kernels, shards(): pl.pallas_call(branch_kernel, out_shape=(jax.ShapeDtypeStruct((chips, row...  4.3 us
    all_to_all x1, waiting for transfers between devices, shards(): lax.all_to_all(acts_copies, 'tensor', 0, 0, axis_index_groups=same_core,...  3.3 us
  transfers between devices with their start and end apart: 6, of which 4 were waited for; matrix products, arithmetic and copies ran while one was open for 0% of the time, Pallas kernels for 17%

profile of v2, /device:TPU:8, one launch (start us, length us, event | category | flops | bytes accessed | tf_op | source)
XLA Modules:
  0.0 63.8 jit_solution(16706479201412333527)
XLA Ops:
  0.6 0.0 copy-start.1
  0.6 1.9 %spread.1 = bf16[8,16,4096]{2,1,0:T(8,128)(2,1)} custom-call(bf16[1,16,4096]{2,1,0:T(8,128)(2,1)} %acts.1), custom_call_target="tpu_custom_call" | custom-call | tf_op jit(solution)/shard_map/spread/pallas_call | solution.py:181
  2.6 6.0 %all-to-all-start.1 = ((bf16[8,16,4096]{2,1,0:T(8,128)(2,1)}), bf16[8,16,4096]{2,1,0:T(8,128)(2,1)S(1)}, u32[]{:S(2)}, u32[]{:S(2)}) async-start(bf16[8,16,4096]{2,1,0:T(8,128)(2,1)} %spread.1), calls=%async_computation.1 | async-start | bytes 2097152 | tf_op jit(solution)/shard_map/all_to_all | solution.py:192
  9.3 0.0 copy-done.1
  9.3 4.3 %branch.1 = (f32[8,16,4096]{2,1,0:T(8,128)S(1)}, s16[4,16,4224]{2,1,0:T(8,128)(2,1)S(1)}, s16[4,16,4224]{2,1,0:T(8,128)(2,1)S(1)}) custom-call(s32[1,64]{1,0:T(1,128)S(1)} %bitcast.7, s32[1,1]{1,0:T(1,128)S(6)} %copy.9.counts, bf16[8,2,16,896]{3,2,1,0:T(8,128)(2,1)} %bitcast.11, bf16[64,128,128]{2,1,0:T(8,128)(2,1)} %bitcast.10), custom_call_target="tpu_custom_call" | custom-call | flops 1024 | bytes 1024 | tf_op jit(solution)/shard_map/branch/pallas_call | solution.py:198
  13.6 1.9 %collective-permute-start = (s16[4,16,4224]{2,1,0:T(8,128)(2,1)S(1)}, s16[4,16,4224]{2,1,0:T(8,128)(2,1)S(1)}, u32[]{:S(2)}, u32[]{:S(2)}) collective-permute-start(s16[4,16,4224]{2,1,0:T(8,128)(2,1)S(1)} %get-tuple-element.14), channel_id=1, source_target_pairs={{0,1},{1,0},{2,3},{3,2},{4,5},{5,4},{6,7},{7,6},{8,9},{9,8},{10,11... | collective-permute-start | bytes 1622024 | tf_op jit(solution)/shard_map/ppermute | solution.py:213
  15.5 2.4 %collective-permute-start.1 = (s16[4,16,4224]{2,1,0:T(8,128)(2,1)S(1)}, s16[4,16,4224]{2,1,0:T(8,128)(2,1)S(1)}, u32[]{:S(2)}, u32[]{:S(2)}) collective-permute-start(s16[4,16,4224]{2,1,0:T(8,128)(2,1)S(1)} %get-tuple-element.15), channel_id=1, source_target_pairs={{0,1},{1,0},{2,3},{3,2},{4,5},{5,4},{6,7},{7,6},{8,9},{9,8},{10,11... | collective-permute-start | bytes 1622024 | tf_op jit(solution)/shard_map/ppermute | solution.py:213
  17.9 0.0 collective-permute-done.refs_0_
  17.9 1.5 %collective-permute-done.1.refs_1_ = s16[4,16,4224]{2,1,0:T(8,128)(2,1)S(1)} collective-permute-done((s16[4,16,4224]{2,1,0:T(8,128)(2,1)S(1)}, s16[4,16,4224]{2,1,0:T(8,128)(2,1)S(1)}, u32[]{:S(2)}, u32[]{:S(2)}) %collective-permute-start.1) | collective-permute-done | bytes 540704 | tf_op jit(solution)/shard_map/ppermute | solution.py:213
  19.5 1.7 %merge.1 = s16[8,16,4224]{2,1,0:T(8,128)(2,1)} custom-call(f32[8,16,4096]{2,1,0:T(8,128)S(1)} %get-tuple-element.13.keep, s16[4,16,4224]{2,1,0:T(8,128)(2,1)S(1)} %collective-permute-done.refs_0_, s16[4,16,4224]{2,1,0:T(8,128)(2,1)S(1)} %collective-permute-done.1.refs_1_), custom_call_target="tpu_custom_call" | custom-call | flops 1024 | bytes 1024 | tf_op jit(solution)/shard_map/merge/pallas_call | solution.py:214
  21.2 3.3 %all-to-all-done.1.a0 = bf16[8,16,4096]{2,1,0:T(8,128)(2,1)S(1)} async-done(((bf16[8,16,4096]{2,1,0:T(8,128)(2,1)}), bf16[8,16,4096]{2,1,0:T(8,128)(2,1)S(1)}, u32[]{:S(2)}, u32[]{:S(2)}) %all-to-all-start.1) | async-done | bytes 1048608 | tf_op jit(solution)/shard_map/all_to_all | solution.py:192
  24.5 1.9 %collective-permute-start.2 = (bf16[8,16,4096]{2,1,0:T(8,128)(2,1)S(1)}, bf16[8,16,4096]{2,1,0:T(8,128)(2,1)S(1)}, u32[]{:S(2)}, u32[]{:S(2)}) collective-permute-start(bf16[8,16,4096]{2,1,0:T(8,128)(2,1)S(1)} %all-to-all-done.1.a0), channel_id=1, source_target_pairs={{0,1},{1,0},{2,3},{3,2},{4,5},{5,4},{6,7},{7,6},{8,9},{9,8},{10,11... | collective-permute-start | bytes 3145736 | tf_op jit(solution)/shard_map/ppermute | solution.py:226
  26.4 4.7 %all-to-all-start = ((s16[8,16,4224]{2,1,0:T(8,128)(2,1)}), s16[8,16,4224]{2,1,0:T(8,128)(2,1)S(1)}, u32[]{:S(2)}, u32[]{:S(2)}) async-start(s16[8,16,4224]{2,1,0:T(8,128)(2,1)} %merge.1), calls=%async_computation | async-start | bytes 2162688 | tf_op jit(solution)/shard_map/all_to_all | solution.py:224
  31.1 0.0 copy-start
  31.1 0.0 collective-permute-done.2.a1
  31.1 4.6 %weight_grads.1 = bf16[64,128,128]{2,1,0:T(8,128)(2,1)} custom-call(s32[1,64]{1,0:T(1,128)S(1)} %bitcast.8, s32[1,1]{1,0:T(1,128)S(6)} %copy.9.counts, bf16[8,16,4096]{2,1,0:T(8,128)(2,1)S(1)} %all-to-all-done.1.a0, bf16[8,16,4096]{2,1,0:T(8,128)(2,1)S(1)} %collective-permute-done.2.a1, bf16[8,2,16,896]{3,2,1,0:T(8,128)(2,1)} %bitcast.12), custom_call_target="tpu_custom_call" | custom-call | flops 1024 | bytes 1024 | tf_op jit(solution)/shard_map/weight_grads/pallas_call | solution.py:227
  35.8 12.3 %all-to-all-done.parts = s16[8,16,4224]{2,1,0:T(8,128)(2,1)S(1)} async-done(((s16[8,16,4224]{2,1,0:T(8,128)(2,1)}), s16[8,16,4224]{2,1,0:T(8,128)(2,1)S(1)}, u32[]{:S(2)}, u32[]{:S(2)}) %all-to-all-start) | async-done | bytes 1081376 | tf_op jit(solution)/shard_map/all_to_all | solution.py:224
  48.1 0.0 copy-done
  48.1 0.3 total.1
  48.5 12.2 %collective-permute-start.3 = (bf16[1,16,4096]{2,1,0:T(8,128)(2,1)S(1)}, bf16[1,16,4096]{2,1,0:T(8,128)(2,1)S(1)}, u32[]{:S(2)}, u32[]{:S(2)}) collective-permute-start(bf16[1,16,4096]{2,1,0:T(8,128)(2,1)S(1)} %total.1), channel_id=1, source_target_pairs={{16,0},{32,16},{48,32},{64,48},{80,64},{96,80},{112,96},{128,112},... | collective-permute-start | bytes 393224 | tf_op jit(solution)/shard_map/ppermute | solution.py:250
  60.7 2.5 %collective-permute-done.3 = bf16[1,16,4096]{2,1,0:T(8,128)(2,1)S(1)} collective-permute-done((bf16[1,16,4096]{2,1,0:T(8,128)(2,1)S(1)}, bf16[1,16,4096]{2,1,0:T(8,128)(2,1)S(1)}, u32[]{:S(2)}, u32[]{:S(2)}) %collective-permute-start.3) | collective-permute-done | bytes 131104 | tf_op jit(solution)/shard_map/ppermute | solution.py:250
  63.2 0.7 %copy.10 = bf16[1,16,4096]{2,1,0:T(8,128)(2,1)} copy(bf16[1,16,4096]{2,1,0:T(8,128)(2,1)S(1)} %collective-permute-done.3) | data formatting | bytes 262144
Async XLA Ops:
  0.6 8.6 %copy-start.1 = (s32[1,1,64]{2,1,0:T(1,128)S(1)}, s32[1,1,64]{2,1,0:T(1,128)}, u32[]{:S(2)}) copy-start(s32[1,1,64]{2,1,0:T(1,128)} %param.10) | copy-start | bytes 772
  2.6 21.9 %all-to-all-start.1 = ((bf16[8,16,4096]{2,1,0:T(8,128)(2,1)}), bf16[8,16,4096]{2,1,0:T(8,128)(2,1)S(1)}, u32[]{:S(2)}, u32[]{:S(2)}) async-start(bf16[8,16,4096]{2,1,0:T(8,128)(2,1)} %spread.1), calls=%async_computation.1 | async-start | bytes 2097152 | tf_op jit(solution)/shard_map/all_to_all | solution.py:192
  13.6 4.3 %collective-permute-start = (s16[4,16,4224]{2,1,0:T(8,128)(2,1)S(1)}, s16[4,16,4224]{2,1,0:T(8,128)(2,1)S(1)}, u32[]{:S(2)}, u32[]{:S(2)}) collective-permute-start(s16[4,16,4224]{2,1,0:T(8,128)(2,1)S(1)} %get-tuple-element.14), channel_id=1, source_target_pairs={{0,1},{1,0},{2,3},{3,2},{4,5},{5,4},{6,7},{7,6},{8,9},{9,8},{10,11... | collective-permute-start | bytes 1622024 | tf_op jit(solution)/shard_map/ppermute | solution.py:213
  15.5 4.0 %collective-permute-start.1 = (s16[4,16,4224]{2,1,0:T(8,128)(2,1)S(1)}, s16[4,16,4224]{2,1,0:T(8,128)(2,1)S(1)}, u32[]{:S(2)}, u32[]{:S(2)}) collective-permute-start(s16[4,16,4224]{2,1,0:T(8,128)(2,1)S(1)} %get-tuple-element.15), channel_id=1, source_target_pairs={{0,1},{1,0},{2,3},{3,2},{4,5},{5,4},{6,7},{7,6},{8,9},{9,8},{10,11... | collective-permute-start | bytes 1622024 | tf_op jit(solution)/shard_map/ppermute | solution.py:213
  24.5 6.7 %collective-permute-start.2 = (bf16[8,16,4096]{2,1,0:T(8,128)(2,1)S(1)}, bf16[8,16,4096]{2,1,0:T(8,128)(2,1)S(1)}, u32[]{:S(2)}, u32[]{:S(2)}) collective-permute-start(bf16[8,16,4096]{2,1,0:T(8,128)(2,1)S(1)} %all-to-all-done.1.a0), channel_id=1, source_target_pairs={{0,1},{1,0},{2,3},{3,2},{4,5},{5,4},{6,7},{7,6},{8,9},{9,8},{10,11... | collective-permute-start | bytes 3145736 | tf_op jit(solution)/shard_map/ppermute | solution.py:226
  26.4 21.7 %all-to-all-start = ((s16[8,16,4224]{2,1,0:T(8,128)(2,1)}), s16[8,16,4224]{2,1,0:T(8,128)(2,1)S(1)}, u32[]{:S(2)}, u32[]{:S(2)}) async-start(s16[8,16,4224]{2,1,0:T(8,128)(2,1)} %merge.1), calls=%async_computation | async-start | bytes 2162688 | tf_op jit(solution)/shard_map/all_to_all | solution.py:224
  31.1 17.0 %copy-start = (bf16[1,16,4096]{2,1,0:T(8,128)(2,1)S(1)}, bf16[1,16,4096]{2,1,0:T(8,128)(2,1)}, u32[]{:S(2)}) copy-start(bf16[1,16,4096]{2,1,0:T(8,128)(2,1)} %param.8) | copy-start | bytes 393220
  48.5 14.7 %collective-permute-start.3 = (bf16[1,16,4096]{2,1,0:T(8,128)(2,1)S(1)}, bf16[1,16,4096]{2,1,0:T(8,128)(2,1)S(1)}, u32[]{:S(2)}, u32[]{:S(2)}) collective-permute-start(bf16[1,16,4096]{2,1,0:T(8,128)(2,1)S(1)} %total.1), channel_id=1, source_target_pairs={{16,0},{32,16},{48,32},{64,48},{80,64},{96,80},{112,96},{128,112},... | collective-permute-start | bytes 393224 | tf_op jit(solution)/shard_map/ppermute | solution.py:250

commit v3 on v2

--- a/solution.py
+++ b/solution.py
@@ -61,7 +61,7 @@
 
 
 def branch_kernel(ids, counts, hidden, tiles, keep, *refs):
-    codes, (give, held, w, sems) = refs[:-4], refs[-4:]
+    codes, (held, give, w, sems) = refs[:-4], refs[-4:]
     share = codes[0].shape[0]
     chips, rows, width = keep.shape
     blocks = width // BLK
@@ -128,38 +128,36 @@
         out[0, :, at] = (residual[:, at].astype(jnp.float32) + value).astype(out.dtype)
 
 
-def weight_kernel(ids, counts, a0, a1, hidden, out, held, sems):
+def weight_kernel(ids, counts, a0, a1, held, out, made, sems):
     chips, rows = a0.shape[:2]
     blocks = a0.shape[-1] // BLK
     slots = out.shape[0]
     live_count = counts[0, 0]
-    copies = hidden_copies(hidden, held, sems)
-    for copy in copies:
+    copies = []
+    for g in range(slots // GROUP):
+        some = pl.ds(g * GROUP, GROUP)
+
+        @pl.when(g * GROUP < live_count)
+        def _(g=g):
+            for j in range(g * GROUP, (g + 1) * GROUP):
+                name = ids[0, j]
+                live = j < live_count
+                c = pl.ds(pl.multiple_of(jnp.where(live, name // blocks, 0) * BLK, BLK), BLK)
+                b = pl.ds(pl.multiple_of(jnp.where(live, name % blocks, 0) * BLK, BLK), BLK)
+                act = jnp.concatenate([a[:, :, b].reshape(chips * rows, BLK) for a in (a0, a1)], axis=0)
+                hid = held[:, :, :, c].reshape(2 * chips * rows, BLK)
+                d = lax.dot_general(act, hid, (((0,), (0,)), ((), ())), preferred_element_type=jnp.float32)
+                made[j] = jnp.where(live, d, 0.0).astype(out.dtype)
+
+        @pl.when(g * GROUP >= live_count)
+        def _(some=some):
+            made[some] = jnp.zeros((GROUP, BLK, BLK), out.dtype)
+
+        copy = pltpu.make_async_copy(made.at[some], out.at[some], sems.at[g])
         copy.start()
+        copies.append(copy)
     for copy in copies:
         copy.wait()
-
-    def some(t, _):
-        for u in range(GROUP):
-            j = t * GROUP + u
-            name = ids[0, j]
-            live = j < live_count
-            c = pl.ds(pl.multiple_of(jnp.where(live, name // blocks, 0) * BLK, BLK), BLK)
-            b = pl.ds(pl.multiple_of(jnp.where(live, name % blocks, 0) * BLK, BLK), BLK)
-            act = jnp.concatenate([a[:, :, b].reshape(chips * rows, BLK) for a in (a0, a1)], axis=0)
-            hid = held[:, :, :, c].reshape(2 * chips * rows, BLK)
-            d = lax.dot_general(act, hid, (((0,), (0,)), ((), ())), preferred_element_type=jnp.float32)
-            out[j] = jnp.where(live, d, 0.0).astype(out.dtype)
-        return 0
-
-    trips = (live_count + GROUP - 1) // GROUP
-    lax.fori_loop(0, trips, some, 0)
-
-    def clear(j, _):
-        out[j] = jnp.zeros((BLK, BLK), out.dtype)
-        return 0
-
-    lax.fori_loop(trips * GROUP, slots, clear, 0)
 
 
 SMEM = pl.BlockSpec(memory_space=pltpu.SMEM)
@@ -195,14 +193,14 @@
     coded = jax.ShapeDtypeStruct((chips, rows, width + BLK), jnp.int16)
     partial = pltpu.VMEM((chips, rows, width), jnp.float32)
     share = jax.ShapeDtypeStruct((chips // PIECES, rows, width + BLK), jnp.int16)
-    keep, *gives = pl.pallas_call(
+    held = jax.ShapeDtypeStruct((2, chips, rows, hidden_width + BLK), jnp.bfloat16)
+    keep, *gives, held = pl.pallas_call(
         branch_kernel,
-        out_shape=(jax.ShapeDtypeStruct((chips, rows, width), jnp.float32),) + (share,) * PIECES,
+        out_shape=(jax.ShapeDtypeStruct((chips, rows, width), jnp.float32),) + (share,) * PIECES + (held,),
         in_specs=[SMEM, SMEM, ANY, ANY],
-        out_specs=(VMEM,) * (1 + PIECES),
+        out_specs=(VMEM,) * (2 + PIECES),
         scratch_shapes=[
             partial,
-            pltpu.VMEM((2, chips, rows, hidden_width + BLK), jnp.bfloat16),
             pltpu.VMEM((slots, BLK, BLK), jnp.bfloat16),
             pltpu.SemaphoreType.DMA((2 + slots // GROUP,)),
         ],
@@ -221,33 +219,56 @@
         cost_estimate=pl.CostEstimate(flops=1 << 10, bytes_accessed=1 << 10, transcendentals=0),
         name="merge",
     )(keep, *gots)
-    parts = lax.all_to_all(sent, "tensor", 0, 0, axis_index_groups=same_core, tiled=True)
-    acts, _ = lax.optimization_barrier((acts, sent))
+    acts, sent = lax.optimization_barrier((acts, sent))
     acts_other = lax.ppermute(acts, "tensor", swap)
+    residual = residual_grad[0]
+    pipes = lax.axis_size("pipe")
+    late = pipes // 2 - 1
+    is_late = lax.axis_index("pipe") == late
+
+    def reduced(sent, residual):
+        parts = lax.all_to_all(sent, "tensor", 0, 0, axis_index_groups=same_core, tiled=True)
+        return pl.pallas_call(
+            total_kernel,
+            out_shape=jax.ShapeDtypeStruct((1, rows, width), jnp.bfloat16),
+            in_specs=[VMEM, VMEM],
+            out_specs=VMEM,
+            compiler_params=PARAMS,
+            name="total",
+        )(parts, residual)
+
+    early = lax.cond(
+        is_late,
+        lambda sent, residual: jnp.zeros((1, rows, width), jnp.bfloat16),
+        reduced,
+        sent,
+        residual,
+    )
+    most = lax.ppermute(early, "pipe", [(i, i - 1) for i in range(1, pipes) if i != late])
+    sent, _ = lax.optimization_barrier((sent, early))
+    behind = lax.cond(
+        is_late,
+        reduced,
+        lambda sent, residual: jnp.zeros((1, rows, width), jnp.bfloat16),
+        sent,
+        residual,
+    )
+    rest = lax.ppermute(behind, "pipe", [(late, late - 1)])
     grads = pl.pallas_call(
         weight_kernel,
         out_shape=jax.ShapeDtypeStruct((slots, BLK, BLK), jnp.bfloat16),
-        in_specs=[SMEM, SMEM, VMEM, VMEM, ANY],
-        out_specs=VMEM,
+        in_specs=[SMEM, SMEM, VMEM, VMEM, VMEM],
+        out_specs=ANY,
         scratch_shapes=[
-            pltpu.VMEM((2, chips, rows, hidden_width), jnp.bfloat16),
-            pltpu.SemaphoreType.DMA((2,)),
+            pltpu.VMEM((slots, BLK, BLK), jnp.bfloat16),
+            pltpu.SemaphoreType.DMA((slots // GROUP,)),
         ],
         compiler_params=PARAMS,
-        cost_estimate=pl.CostEstimate(flops=1 << 10, bytes_accessed=1 << 10, transcendentals=0),
+        cost_estimate=pl.CostEstimate(flops=4 << 30, bytes_accessed=6 << 20, transcendentals=0),
         name="weight_grads",
-    )(tile_ids[0], tile_counts, acts, acts_other, hidden)
-    parts, grads = lax.optimization_barrier((parts, grads))
-    total = pl.pallas_call(
-        total_kernel,
-        out_shape=jax.ShapeDtypeStruct((1, rows, width), jnp.bfloat16),
-        in_specs=[VMEM, VMEM],
-        out_specs=VMEM,
-        compiler_params=PARAMS,
-        name="total",
-    )(parts, residual_grad[0])
-    pipes = lax.axis_size("pipe")
-    received = lax.ppermute(total, "pipe", [(i, i - 1) for i in range(1, pipes)])
+    )(tile_ids[0], tile_counts, acts, lax.optimization_barrier((acts_other, behind))[0], held)
+    rest, most, grads = lax.optimization_barrier((rest, most, grads))
+    received = jnp.where(lax.axis_index("pipe") == late - 1, rest, most)
     return received, grads[None, None]
 
 

time: 64.2 us -> 62 us (0.966)
  the two profiles are of different devices: /device:TPU:8 before, /device:TPU:480 now
where the time goes in v3:
time: 62 us; the launch traced here: 61.7 us
  blocking collectives  22.5 us (36%)
  starting transfers between devices  19.5 us (31%)
  Pallas kernels  13.3 us (21%)
  waiting for transfers between devices  4.18 us (7%)
  between operations  1.42 us (2%)
  other arithmetic  0.68 us (1%)
    all_to_all x1, blocking collectives, reduced(): lax.all_to_all(sent, 'tensor', 0, 0, axis_index_groups=same_core, tiled=T...  22.5 us
    all_to_all x1, starting transfers between devices, shards(): lax.all_to_all(acts_copies, 'tensor', 0, 0, axis_index_groups=same_core,...  6.94 us
    ppermute x1, starting transfers between devices, shards(): rest = lax.ppermute(behind, 'pipe', [(late, late - 1)])  5.05 us
    pallas_call x1, Pallas kernels, shards(): pl.pallas_call(branch_kernel, out_shape=(jax.ShapeDtypeStruct((chips, row...  4.95 us
    pallas_call x1, Pallas kernels, shards(): pl.pallas_call(weight_kernel, out_shape=jax.ShapeDtypeStruct((slots, BLK,...  4.33 us
    ppermute x2, starting transfers between devices, shards(): gots = [lax.ppermute(give, 'tensor', swap) for give in gives]  4.33 us
    all_to_all x1, waiting for transfers between devices, shards(): lax.all_to_all(acts_copies, 'tensor', 0, 0, axis_index_groups=same_core,...  2.64 us
    pallas_call x1, Pallas kernels, shards(): pl.pallas_call(spread_kernel, out_shape=jax.ShapeDtypeStruct((chips, rows...  1.95 us
  transfers between devices with their start and end apart: 6, of which 2 were waited for; matrix products, arithmetic and copies ran while one was open for 0% of the time, Pallas kernels for 18%

profile of v3, /device:TPU:480, one launch (start us, length us, event | category | flops | bytes accessed | tf_op | source)
XLA Modules:
  0.0 61.7 jit_solution(8823583938685153364)
XLA Ops:
  0.6 0.0 copy-start
  0.6 2.0 %spread.1 = bf16[8,16,4096]{2,1,0:T(8,128)(2,1)} custom-call(bf16[1,16,4096]{2,1,0:T(8,128)(2,1)} %acts.1), custom_call_target="tpu_custom_call" | custom-call | tf_op jit(solution)/shard_map/spread/pallas_call | solution.py:179
  2.6 6.9 %all-to-all-start.2 = ((bf16[8,16,4096]{2,1,0:T(8,128)(2,1)}), bf16[8,16,4096]{2,1,0:T(8,128)(2,1)S(1)}, u32[]{:S(2)}, u32[]{:S(2)}) async-start(bf16[8,16,4096]{2,1,0:T(8,128)(2,1)} %spread.1), calls=%async_computation.2 | async-start | bytes 2097152 | tf_op jit(solution)/shard_map/all_to_all | solution.py:190
  10.2 0.0 copy-done
  10.2 5.0 %branch.1 = (f32[8,16,4096]{2,1,0:T(8,128)S(1)}, s16[4,16,4224]{2,1,0:T(8,128)(2,1)S(1)}, s16[4,16,4224]{2,1,0:T(8,128)(2,1)S(1)}, bf16[2,8,16,1024]{3,2,1,0:T(8,128)(2,1)S(1)}) custom-call(s32[1,64]{1,0:T(1,128)S(1)} %bitcast.6, s32[1,1]{1,0:T(1,128)S(6)} %copy.12.counts, bf16[8,2,16,896]{3,2,1,0:T(8,128)(2,1)} %bitcast.11, bf16[64,128,128]{2,1,0:T(8,128)(2,1)} %bitcast.8), custom_call_target="tpu_custom_call" | custom-call | flops 1024 | bytes 1024 | tf_op jit(solution)/shard_map/branch/pallas_call | solution.py:197
  15.2 1.9 %collective-permute-start = (s16[4,16,4224]{2,1,0:T(8,128)(2,1)S(1)}, s16[4,16,4224]{2,1,0:T(8,128)(2,1)S(1)}, u32[]{:S(2)}, u32[]{:S(2)}) collective-permute-start(s16[4,16,4224]{2,1,0:T(8,128)(2,1)S(1)} %get-tuple-element.38), channel_id=1, source_target_pairs={{0,1},{1,0},{2,3},{3,2},{4,5},{5,4},{6,7},{7,6},{8,9},{9,8},{10,11... | collective-permute-start | bytes 1622024 | tf_op jit(solution)/shard_map/ppermute | solution.py:211
  17.1 2.4 %collective-permute-start.1 = (s16[4,16,4224]{2,1,0:T(8,128)(2,1)S(1)}, s16[4,16,4224]{2,1,0:T(8,128)(2,1)S(1)}, u32[]{:S(2)}, u32[]{:S(2)}) collective-permute-start(s16[4,16,4224]{2,1,0:T(8,128)(2,1)S(1)} %get-tuple-element.39), channel_id=1, source_target_pairs={{0,1},{1,0},{2,3},{3,2},{4,5},{5,4},{6,7},{7,6},{8,9},{9,8},{10,11... | collective-permute-start | bytes 1622024 | tf_op jit(solution)/shard_map/ppermute | solution.py:211
  19.5 0.0 collective-permute-done.refs_0_
  19.5 1.5 %collective-permute-done.1.refs_1_ = s16[4,16,4224]{2,1,0:T(8,128)(2,1)S(1)} collective-permute-done((s16[4,16,4224]{2,1,0:T(8,128)(2,1)S(1)}, s16[4,16,4224]{2,1,0:T(8,128)(2,1)S(1)}, u32[]{:S(2)}, u32[]{:S(2)}) %collective-permute-start.1) | collective-permute-done | bytes 540704 | tf_op jit(solution)/shard_map/ppermute | solution.py:211
  21.0 0.0 copy-start.1
  21.0 1.7 %merge.1 = s16[8,16,4224]{2,1,0:T(8,128)(2,1)} custom-call(f32[8,16,4096]{2,1,0:T(8,128)S(1)} %get-tuple-element.37.keep, s16[4,16,4224]{2,1,0:T(8,128)(2,1)S(1)} %collective-permute-done.refs_0_, s16[4,16,4224]{2,1,0:T(8,128)(2,1)S(1)} %collective-permute-done.1.refs_1_), custom_call_target="tpu_custom_call" | custom-call | flops 1024 | bytes 1024 | tf_op jit(solution)/shard_map/merge/pallas_call | solution.py:212
  22.7 2.6 %all-to-all-done.2.a0 = bf16[8,16,4096]{2,1,0:T(8,128)(2,1)S(1)} async-done(((bf16[8,16,4096]{2,1,0:T(8,128)(2,1)}), bf16[8,16,4096]{2,1,0:T(8,128)(2,1)S(1)}, u32[]{:S(2)}, u32[]{:S(2)}) %all-to-all-start.2) | async-done | bytes 1048608 | tf_op jit(solution)/shard_map/all_to_all | solution.py:190
  25.4 1.9 %collective-permute-start.4 = (bf16[8,16,4096]{2,1,0:T(8,128)(2,1)S(1)}, bf16[8,16,4096]{2,1,0:T(8,128)(2,1)S(1)}, u32[]{:S(2)}, u32[]{:S(2)}) collective-permute-start(bf16[8,16,4096]{2,1,0:T(8,128)(2,1)S(1)} %all-to-all-done.2.a0), channel_id=1, source_target_pairs={{0,1},{1,0},{2,3},{3,2},{4,5},{5,4},{6,7},{7,6},{8,9},{9,8},{10,11... | collective-permute-start | bytes 3145736 | tf_op jit(solution)/shard_map/ppermute | solution.py:223
  27.3 0.0 copy-done.1
  27.4 1.3 %collective-permute-start.3 = (bf16[1,16,4096]{2,1,0:T(8,128)(2,1)S(1)}, bf16[1,16,4096]{2,1,0:T(8,128)(2,1)S(1)}, u32[]{:S(2)}, u32[]{:S(2)}) collective-permute-start(bf16[1,16,4096]{2,1,0:T(8,128)(2,1)S(1)} %get-tuple-element.48), channel_id=1, source_target_pairs={{16,0},{32,16},{48,32},{64,48},{80,64},{96,80},{112,96},{128,112},... | collective-permute-start | bytes 393224 | tf_op jit(solution)/shard_map/ppermute | solution.py:247
  28.7 22.9 %conditional.3 = (bf16[1,16,4096]{2,1,0:T(8,128)(2,1)S(1)}) conditional(s32[]{:T(128)} %convert_element_type.4, () %tuple.25, (s16[8,16,4224]{2,1,0:T(8,128)(2,1)}, bf16[16,4096]{1,0:T(8,128)(2,1)S(1)}) %tuple.40), branch_computations={%region_2.0_spmd, %region_3.0_spmd} | conditional | bytes 2162696 | solution.py:249
  28.7 22.5 %all_to_all.14.parts = s16[8,16,4224]{2,1,0:T(8,128)(2,1)S(1)} all-to-all(s16[8,16,4224]{2,1,0:T(8,128)(2,1)} %get-tuple-element.16), channel_id=1, replica_groups={{0,2,4,6,8,10,12,14},{1,3,5,7,9,11,13,15},{16,18,20,22,24,26,28,30},{17..., dimensions={0} | all-to-all | bytes 2162688 | tf_op jit(solution)/shard_map/cond/branch_1_fun/all_to_all | solution.py:230
  51.2 0.3 total.3
  51.5 5.1 %collective-permute-start.2 = (bf16[1,16,4096]{2,1,0:T(8,128)(2,1)S(1)}, bf16[1,16,4096]{2,1,0:T(8,128)(2,1)S(1)}, u32[]{:S(2)}, u32[]{:S(2)}) collective-permute-start(bf16[1,16,4096]{2,1,0:T(8,128)(2,1)S(1)} %get-tuple-element.49), channel_id=1, source_target_pairs={{240,224},{241,225},{242,226},{243,227},{244,228},{245,229},{246,2... | collective-permute-start | bytes 393224 | tf_op jit(solution)/shard_map/ppermute | solution.py:256
  56.6 0.0 collective-permute-done.4.a1
  56.6 4.3 %weight_grads.1 = bf16[64,128,128]{2,1,0:T(8,128)(2,1)} custom-call(s32[1,64]{1,0:T(1,128)S(1)} %bitcast.7, s32[1,1]{1,0:T(1,128)S(6)} %copy.12.counts, bf16[8,16,4096]{2,1,0:T(8,128)(2,1)S(1)} %all-to-all-done.2.a0, bf16[8,16,4096]{2,1,0:T(8,128)(2,1)S(1)} %collective-permute-done.4.a1, bf16[2,8,16,1024]{3,2,1,0:T(8,128)(2,1)S(1)} %get-tuple-element.44.held), custom_call_target="tpu_custom_call" | custom-call | flops 4294967296 | bytes 6291456 | tf_op jit(solution)/shard_map/weight_grads/pallas_call | solution.py:257
  61.0 0.0 collective-permute-done.2
  61.0 0.0 collective-permute-done.3
  61.0 0.7 %broadcast_select_fusion = bf16[1,16,4096]{2,1,0:T(8,128)(2,1)} fusion(bf16[1,16,4096]{2,1,0:T(8,128)(2,1)S(1)} %collective-permute-done.2, bf16[1,16,4096]{2,1,0:T(8,128)(2,1)S(1)} %collective-permute-done.3, pred[]{:T(512)S(6)} %eq.6), kind=kLoop, calls=%fused_computation | loop fusion | flops 65536 | bytes 393217 | tf_op jit(solution)/shard_map/jit(_where)/select_n | solution.py:271
  (2 shorter events, 0.0 us)
Async XLA Ops:
  0.6 9.6 %copy-start = (s32[1,1,64]{2,1,0:T(1,128)S(1)}, s32[1,1,64]{2,1,0:T(1,128)}, u32[]{:S(2)}) copy-start(s32[1,1,64]{2,1,0:T(1,128)} %param.14) | copy-start | bytes 772
  2.6 22.8 %all-to-all-start.2 = ((bf16[8,16,4096]{2,1,0:T(8,128)(2,1)}), bf16[8,16,4096]{2,1,0:T(8,128)(2,1)S(1)}, u32[]{:S(2)}, u32[]{:S(2)}) async-start(bf16[8,16,4096]{2,1,0:T(8,128)(2,1)} %spread.1), calls=%async_computation.2 | async-start | bytes 2097152 | tf_op jit(solution)/shard_map/all_to_all | solution.py:190
  15.2 4.3 %collective-permute-start = (s16[4,16,4224]{2,1,0:T(8,128)(2,1)S(1)}, s16[4,16,4224]{2,1,0:T(8,128)(2,1)S(1)}, u32[]{:S(2)}, u32[]{:S(2)}) collective-permute-start(s16[4,16,4224]{2,1,0:T(8,128)(2,1)S(1)} %get-tuple-element.38), channel_id=1, source_target_pairs={{0,1},{1,0},{2,3},{3,2},{4,5},{5,4},{6,7},{7,6},{8,9},{9,8},{10,11... | collective-permute-start | bytes 1622024 | tf_op jit(solution)/shard_map/ppermute | solution.py:211
  17.1 4.0 %collective-permute-start.1 = (s16[4,16,4224]{2,1,0:T(8,128)(2,1)S(1)}, s16[4,16,4224]{2,1,0:T(8,128)(2,1)S(1)}, u32[]{:S(2)}, u32[]{:S(2)}) collective-permute-start(s16[4,16,4224]{2,1,0:T(8,128)(2,1)S(1)} %get-tuple-element.39), channel_id=1, source_target_pairs={{0,1},{1,0},{2,3},{3,2},{4,5},{5,4},{6,7},{7,6},{8,9},{9,8},{10,11... | collective-permute-start | bytes 1622024 | tf_op jit(solution)/shard_map/ppermute | solution.py:211
  21.0 6.3 %copy-start.1 = (bf16[1,16,4096]{2,1,0:T(8,128)(2,1)S(1)}, bf16[1,16,4096]{2,1,0:T(8,128)(2,1)}, u32[]{:S(2)}) copy-start(bf16[1,16,4096]{2,1,0:T(8,128)(2,1)} %param.12) | copy-start | bytes 393220
  25.4 31.2 %collective-permute-start.4 = (bf16[8,16,4096]{2,1,0:T(8,128)(2,1)S(1)}, bf16[8,16,4096]{2,1,0:T(8,128)(2,1)S(1)}, u32[]{:S(2)}, u32[]{:S(2)}) collective-permute-start(bf16[8,16,4096]{2,1,0:T(8,128)(2,1)S(1)} %all-to-all-done.2.a0), channel_id=1, source_target_pairs={{0,1},{1,0},{2,3},{3,2},{4,5},{5,4},{6,7},{7,6},{8,9},{9,8},{10,11... | collective-permute-start | bytes 3145736 | tf_op jit(solution)/shard_map/ppermute | solution.py:223
  27.4 33.6 %collective-permute-start.3 = (bf16[1,16,4096]{2,1,0:T(8,128)(2,1)S(1)}, bf16[1,16,4096]{2,1,0:T(8,128)(2,1)S(1)}, u32[]{:S(2)}, u32[]{:S(2)}) collective-permute-start(bf16[1,16,4096]{2,1,0:T(8,128)(2,1)S(1)} %get-tuple-element.48), channel_id=1, source_target_pairs={{16,0},{32,16},{48,32},{64,48},{80,64},{96,80},{112,96},{128,112},... | collective-permute-start | bytes 393224 | tf_op jit(solution)/shard_map/ppermute | solution.py:247
  51.5 9.4 %collective-permute-start.2 = (bf16[1,16,4096]{2,1,0:T(8,128)(2,1)S(1)}, bf16[1,16,4096]{2,1,0:T(8,128)(2,1)S(1)}, u32[]{:S(2)}, u32[]{:S(2)}) collective-permute-start(bf16[1,16,4096]{2,1,0:T(8,128)(2,1)S(1)} %get-tuple-element.49), channel_id=1, source_target_pairs={{240,224},{241,225},{242,226},{243,227},{244,228},{245,229},{246,2... | collective-permute-start | bytes 393224 | tf_op jit(solution)/shard_map/ppermute | solution.py:256

commit v4 on v3

--- a/solution.py
+++ b/solution.py
@@ -61,7 +61,7 @@
 
 
 def branch_kernel(ids, counts, hidden, tiles, keep, *refs):
-    codes, (held, give, w, sems) = refs[:-4], refs[-4:]
+    codes, (turned, held, give, w, sems) = refs[:-5], refs[-5:]
     share = codes[0].shape[0]
     chips, rows, width = keep.shape
     blocks = width // BLK
@@ -81,6 +81,9 @@
     give[...] = jnp.zeros_like(give)
     for copy in copies:
         copy.wait()
+    for c in range(empty):
+        at = slice(c * BLK, (c + 1) * BLK)
+        turned[at, :] = held[:, :, :, at].reshape(2 * chips * rows, BLK).T
     for g in range(parts):
         tile_copies[g].wait()
 
@@ -105,16 +108,21 @@
 
 
 def merge_kernel(keep, *refs):
-    gots, (out, both) = refs[:-2], refs[-2:]
+    gots, (out, both, coded, sems) = refs[:-4], refs[-4:]
     chips, rows, width = keep.shape
     share = gots[0].shape[0]
+    copies = []
     for i in range(chips):
         got, g = gots[i // share], i % share
         scale = decode_scale(got[g, :, width:])
         for k in range(width // BLK):
             at = slice(k * BLK, (k + 1) * BLK)
             both[i, :, at] = keep[i, :, at] + got[g, :, at].astype(jnp.int32).astype(jnp.float32) * scale
-        encode_rows(lambda lo, hi, i=i: both[i, :, lo:hi], i, out)
+        encode_rows(lambda lo, hi, i=i: both[i, :, lo:hi], i, coded)
+        copies.append(pltpu.make_async_copy(coded.at[i], out.at[i], sems.at[i]))
+        copies[-1].start()
+    for copy in copies:
+        copy.wait()
 
 
 def total_kernel(parts, residual, out):
@@ -128,7 +136,7 @@
         out[0, :, at] = (residual[:, at].astype(jnp.float32) + value).astype(out.dtype)
 
 
-def weight_kernel(ids, counts, a0, a1, held, out, made, sems):
+def weight_kernel(ids, counts, a0, a1, turned, out, made, sems):
     chips, rows = a0.shape[:2]
     blocks = a0.shape[-1] // BLK
     slots = out.shape[0]
@@ -145,9 +153,8 @@
                 c = pl.ds(pl.multiple_of(jnp.where(live, name // blocks, 0) * BLK, BLK), BLK)
                 b = pl.ds(pl.multiple_of(jnp.where(live, name % blocks, 0) * BLK, BLK), BLK)
                 act = jnp.concatenate([a[:, :, b].reshape(chips * rows, BLK) for a in (a0, a1)], axis=0)
-                hid = held[:, :, :, c].reshape(2 * chips * rows, BLK)
-                d = lax.dot_general(act, hid, (((0,), (0,)), ((), ())), preferred_element_type=jnp.float32)
-                made[j] = jnp.where(live, d, 0.0).astype(out.dtype)
+                d = jnp.dot(turned[c, :], act, preferred_element_type=jnp.float32)
+                made[j] = jnp.where(live, d, 0.0).astype(out.dtype).T
 
         @pl.when(g * GROUP >= live_count)
         def _(some=some):
@@ -193,13 +200,14 @@
     coded = jax.ShapeDtypeStruct((chips, rows, width + BLK), jnp.int16)
     partial = pltpu.VMEM((chips, rows, width), jnp.float32)
     share = jax.ShapeDtypeStruct((chips // PIECES, rows, width + BLK), jnp.int16)
-    held = jax.ShapeDtypeStruct((2, chips, rows, hidden_width + BLK), jnp.bfloat16)
-    keep, *gives, held = pl.pallas_call(
+    turned = jax.ShapeDtypeStruct((hidden_width, 2 * chips * rows), jnp.bfloat16)
+    keep, *gives, turned = pl.pallas_call(
         branch_kernel,
-        out_shape=(jax.ShapeDtypeStruct((chips, rows, width), jnp.float32),) + (share,) * PIECES + (held,),
+        out_shape=(jax.ShapeDtypeStruct((chips, rows, width), jnp.float32),) + (share,) * PIECES + (turned,),
         in_specs=[SMEM, SMEM, ANY, ANY],
         out_specs=(VMEM,) * (2 + PIECES),
         scratch_shapes=[
+            pltpu.VMEM((2, chips, rows, hidden_width + BLK), jnp.bfloat16),
             partial,
             pltpu.VMEM((slots, BLK, BLK), jnp.bfloat16),
             pltpu.SemaphoreType.DMA((2 + slots // GROUP,)),
@@ -213,8 +221,8 @@
         merge_kernel,
         out_shape=coded,
         in_specs=[VMEM] * (1 + PIECES),
-        out_specs=VMEM,
-        scratch_shapes=[partial],
+        out_specs=ANY,
+        scratch_shapes=[partial, pltpu.VMEM(coded.shape, jnp.int16), pltpu.SemaphoreType.DMA((chips,))],
         compiler_params=PARAMS,
         cost_estimate=pl.CostEstimate(flops=1 << 10, bytes_accessed=1 << 10, transcendentals=0),
         name="merge",
@@ -244,7 +252,7 @@
         sent,
         residual,
     )
-    most = lax.ppermute(early, "pipe", [(i, i - 1) for i in range(1, pipes) if i != late])
+    over = lax.ppermute(early, "pipe", [(late + 1, late)])
     sent, _ = lax.optimization_barrier((sent, early))
     behind = lax.cond(
         is_late,
@@ -253,6 +261,8 @@
         sent,
         residual,
     )
+    behind, early = lax.optimization_barrier((behind, early))
+    most = lax.ppermute(early, "pipe", [(i, i - 1) for i in range(1, pipes) if i not in (late, late + 1)])
     rest = lax.ppermute(behind, "pipe", [(late, late - 1)])
     grads = pl.pallas_call(
         weight_kernel,
@@ -266,9 +276,10 @@
         compiler_params=PARAMS,
         cost_estimate=pl.CostEstimate(flops=4 << 30, bytes_accessed=6 << 20, transcendentals=0),
         name="weight_grads",
-    )(tile_ids[0], tile_counts, acts, lax.optimization_barrier((acts_other, behind))[0], held)
+    )(tile_ids[0], tile_counts, acts, lax.optimization_barrier((acts_other, behind))[0], turned)
     rest, most, grads = lax.optimization_barrier((rest, most, grads))
-    received = jnp.where(lax.axis_index("pipe") == late - 1, rest, most)
+    place = lax.axis_index("pipe")
+    received = jnp.where(place == late, over, jnp.where(place == late - 1, rest, most))
     return received, grads[None, None]
 
 

time: 62 us -> 60.9 us (0.982)
  the two profiles are of different devices: /device:TPU:480 before, /device:TPU:96 now
where the time goes in v4:
time: 60.9 us; the launch traced here: 60.4 us
  blocking collectives  22.5 us (37%)
  starting transfers between devices  16.5 us (27%)
  Pallas kernels  11.4 us (19%)
  waiting for transfers between devices  7.77 us (13%)
  between operations  1.44 us (2%)
  other arithmetic  0.68 us (1%)
    all_to_all x1, blocking collectives, reduced(): lax.all_to_all(sent, 'tensor', 0, 0, axis_index_groups=same_core, tiled=T...  22.5 us
    all_to_all x1, starting transfers between devices, shards(): lax.all_to_all(acts_copies, 'tensor', 0, 0, axis_index_groups=same_core,...  6.94 us
    pallas_call x1, Pallas kernels, shards(): pl.pallas_call(branch_kernel, out_shape=(jax.ShapeDtypeStruct((chips, row...  4.36 us
    ppermute x2, starting transfers between devices, shards(): gots = [lax.ppermute(give, 'tensor', swap) for give in gives]  4.33 us
    all_to_all x1, waiting for transfers between devices, shards(): lax.all_to_all(acts_copies, 'tensor', 0, 0, axis_index_groups=same_core,...  3.48 us
    pallas_call x1, Pallas kernels, shards(): pl.pallas_call(weight_kernel, out_shape=jax.ShapeDtypeStruct((slots, BLK,...  3.27 us
    ppermute x1, waiting for transfers between devices, shards(): lax.ppermute(early, 'pipe', [(i, i - 1) for i in range(1, pipes) if i not...  2.75 us
    ppermute x1, starting transfers between devices, shards(): lax.ppermute(early, 'pipe', [(i, i - 1) for i in range(1, pipes) if i not...  2.02 us
  transfers between devices with their start and end apart: 7, of which 3 were waited for; matrix products, arithmetic and copies ran while one was open for 0% of the time, Pallas kernels for 16%

profile of v4, /device:TPU:96, one launch (start us, length us, event | category | flops | bytes accessed | tf_op | source)
XLA Modules:
  0.0 60.4 jit_solution(7317767604161987832)
XLA Ops:
  0.6 0.0 copy-start
  0.6 2.0 %spread.1 = bf16[8,16,4096]{2,1,0:T(8,128)(2,1)} custom-call(bf16[1,16,4096]{2,1,0:T(8,128)(2,1)} %acts.1), custom_call_target="tpu_custom_call" | custom-call | tf_op jit(solution)/shard_map/spread/pallas_call | solution.py:186
  2.6 6.9 %all-to-all-start.2 = ((bf16[8,16,4096]{2,1,0:T(8,128)(2,1)}), bf16[8,16,4096]{2,1,0:T(8,128)(2,1)S(1)}, u32[]{:S(2)}, u32[]{:S(2)}) async-start(bf16[8,16,4096]{2,1,0:T(8,128)(2,1)} %spread.1), calls=%async_computation.2 | async-start | bytes 2097152 | tf_op jit(solution)/shard_map/all_to_all | solution.py:197
  10.2 0.0 copy-done
  10.2 4.4 %branch.1 = (f32[8,16,4096]{2,1,0:T(8,128)S(1)}, s16[4,16,4224]{2,1,0:T(8,128)(2,1)S(1)}, s16[4,16,4224]{2,1,0:T(8,128)(2,1)S(1)}, bf16[896,256]{1,0:T(8,128)(2,1)S(1)}) custom-call(s32[1,64]{1,0:T(1,128)S(1)} %bitcast.6, s32[1,1]{1,0:T(1,128)S(6)} %copy.12.counts, bf16[8,2,16,896]{3,2,1,0:T(8,128)(2,1)} %bitcast.11, bf16[64,128,128]{2,1,0:T(8,128)(2,1)} %bitcast.8), custom_call_target="tpu_custom_call" | custom-call | flops 1024 | bytes 1024 | tf_op jit(solution)/shard_map/branch/pallas_call | solution.py:204
  14.6 1.9 %collective-permute-start = (s16[4,16,4224]{2,1,0:T(8,128)(2,1)S(1)}, s16[4,16,4224]{2,1,0:T(8,128)(2,1)S(1)}, u32[]{:S(2)}, u32[]{:S(2)}) collective-permute-start(s16[4,16,4224]{2,1,0:T(8,128)(2,1)S(1)} %get-tuple-element.40), channel_id=1, source_target_pairs={{0,1},{1,0},{2,3},{3,2},{4,5},{5,4},{6,7},{7,6},{8,9},{9,8},{10,11... | collective-permute-start | bytes 1622024 | tf_op jit(solution)/shard_map/ppermute | solution.py:219
  16.5 2.4 %collective-permute-start.1 = (s16[4,16,4224]{2,1,0:T(8,128)(2,1)S(1)}, s16[4,16,4224]{2,1,0:T(8,128)(2,1)S(1)}, u32[]{:S(2)}, u32[]{:S(2)}) collective-permute-start(s16[4,16,4224]{2,1,0:T(8,128)(2,1)S(1)} %get-tuple-element.41), channel_id=1, source_target_pairs={{0,1},{1,0},{2,3},{3,2},{4,5},{5,4},{6,7},{7,6},{8,9},{9,8},{10,11... | collective-permute-start | bytes 1622024 | tf_op jit(solution)/shard_map/ppermute | solution.py:219
  18.9 0.0 collective-permute-done.refs_0_
  18.9 1.5 %collective-permute-done.1.refs_1_ = s16[4,16,4224]{2,1,0:T(8,128)(2,1)S(1)} collective-permute-done((s16[4,16,4224]{2,1,0:T(8,128)(2,1)S(1)}, s16[4,16,4224]{2,1,0:T(8,128)(2,1)S(1)}, u32[]{:S(2)}, u32[]{:S(2)}) %collective-permute-start.1) | collective-permute-done | bytes 540704 | tf_op jit(solution)/shard_map/ppermute | solution.py:219
  20.5 1.4 %merge.1 = s16[8,16,4224]{2,1,0:T(8,128)(2,1)} custom-call(f32[8,16,4096]{2,1,0:T(8,128)S(1)} %get-tuple-element.39.keep, s16[4,16,4224]{2,1,0:T(8,128)(2,1)S(1)} %collective-permute-done.refs_0_, s16[4,16,4224]{2,1,0:T(8,128)(2,1)S(1)} %collective-permute-done.1.refs_1_), custom_call_target="tpu_custom_call" | custom-call | flops 1024 | bytes 1024 | tf_op jit(solution)/shard_map/merge/pallas_call | solution.py:220
  21.9 3.5 %all-to-all-done.2.a0 = bf16[8,16,4096]{2,1,0:T(8,128)(2,1)S(1)} async-done(((bf16[8,16,4096]{2,1,0:T(8,128)(2,1)}), bf16[8,16,4096]{2,1,0:T(8,128)(2,1)S(1)}, u32[]{:S(2)}, u32[]{:S(2)}) %all-to-all-start.2) | async-done | bytes 1048608 | tf_op jit(solution)/shard_map/all_to_all | solution.py:197
  25.4 1.9 %collective-permute-start.5 = (bf16[8,16,4096]{2,1,0:T(8,128)(2,1)S(1)}, bf16[8,16,4096]{2,1,0:T(8,128)(2,1)S(1)}, u32[]{:S(2)}, u32[]{:S(2)}) collective-permute-start(bf16[8,16,4096]{2,1,0:T(8,128)(2,1)S(1)} %all-to-all-done.2.a0), channel_id=1, source_target_pairs={{0,1},{1,0},{2,3},{3,2},{4,5},{5,4},{6,7},{7,6},{8,9},{9,8},{10,11... | collective-permute-start | bytes 3145736 | tf_op jit(solution)/shard_map/ppermute | solution.py:231
  27.3 22.9 %conditional.2 = (bf16[1,16,4096]{2,1,0:T(8,128)(2,1)S(1)}) conditional(s32[]{:T(128)} %convert_element_type.4, (s16[8,16,4224]{2,1,0:T(8,128)(2,1)}, bf16[16,4096]{1,0:T(8,128)(2,1)S(1)}) %tuple.41, () %tuple.29), branch_computations={%region_0.0_spmd, %region_1.0_spmd} | conditional | bytes 2162696 | solution.py:248
  27.4 22.5 %all_to_all.13.parts = s16[8,16,4224]{2,1,0:T(8,128)(2,1)S(1)} all-to-all(s16[8,16,4224]{2,1,0:T(8,128)(2,1)} %get-tuple-element.11), channel_id=1, replica_groups={{0,2,4,6,8,10,12,14},{1,3,5,7,9,11,13,15},{16,18,20,22,24,26,28,30},{17..., dimensions={0} | all-to-all | bytes 2162688 | tf_op jit(solution)/shard_map/cond/branch_0_fun/all_to_all | solution.py:238
  49.9 0.3 total.2
  50.2 0.7 %collective-permute-start.2 = (bf16[1,16,4096]{2,1,0:T(8,128)(2,1)S(1)}, bf16[1,16,4096]{2,1,0:T(8,128)(2,1)S(1)}, u32[]{:S(2)}, u32[]{:S(2)}) collective-permute-start(bf16[1,16,4096]{2,1,0:T(8,128)(2,1)S(1)} %get-tuple-element.52), channel_id=1, source_target_pairs={{256,240},{257,241},{258,242},{259,243},{260,244},{261,245},{262,2... | collective-permute-start | bytes 393224 | tf_op jit(solution)/shard_map/ppermute | solution.py:255
  50.9 0.7 %collective-permute-start.3 = (bf16[1,16,4096]{2,1,0:T(8,128)(2,1)S(1)}, bf16[1,16,4096]{2,1,0:T(8,128)(2,1)S(1)}, u32[]{:S(2)}, u32[]{:S(2)}) collective-permute-start(bf16[1,16,4096]{2,1,0:T(8,128)(2,1)S(1)} %get-tuple-element.53), channel_id=1, source_target_pairs={{240,224},{241,225},{242,226},{243,227},{244,228},{245,229},{246,2... | collective-permute-start | bytes 393224 | tf_op jit(solution)/shard_map/ppermute | solution.py:266
  51.6 2.0 %collective-permute-start.4 = (bf16[1,16,4096]{2,1,0:T(8,128)(2,1)S(1)}, bf16[1,16,4096]{2,1,0:T(8,128)(2,1)S(1)}, u32[]{:S(2)}, u32[]{:S(2)}) collective-permute-start(bf16[1,16,4096]{2,1,0:T(8,128)(2,1)S(1)} %get-tuple-element.52), channel_id=1, source_target_pairs={{16,0},{32,16},{48,32},{64,48},{80,64},{96,80},{112,96},{128,112},... | collective-permute-start | bytes 393224 | tf_op jit(solution)/shard_map/ppermute | solution.py:265
  53.6 0.0 collective-permute-done.5.a1
  53.6 3.3 %weight_grads.1 = bf16[64,128,128]{2,1,0:T(8,128)(2,1)} custom-call(s32[1,64]{1,0:T(1,128)S(1)} %bitcast.7, s32[1,1]{1,0:T(1,128)S(6)} %copy.12.counts, bf16[8,16,4096]{2,1,0:T(8,128)(2,1)S(1)} %all-to-all-done.2.a0, bf16[8,16,4096]{2,1,0:T(8,128)(2,1)S(1)} %collective-permute-done.5.a1, bf16[896,256]{1,0:T(8,128)(2,1)S(1)} %get-tuple-element.48.turned), custom_call_target="tpu_custom_call" | custom-call | flops 4294967296 | bytes 6291456 | tf_op jit(solution)/shard_map/weight_grads/pallas_call | solution.py:267
  56.9 0.0 collective-permute-done.3
  56.9 2.8 %collective-permute-done.4 = bf16[1,16,4096]{2,1,0:T(8,128)(2,1)S(1)} collective-permute-done((bf16[1,16,4096]{2,1,0:T(8,128)(2,1)S(1)}, bf16[1,16,4096]{2,1,0:T(8,128)(2,1)S(1)}, u32[]{:S(2)}, u32[]{:S(2)}) %collective-permute-start.4) | collective-permute-done | bytes 131104 | tf_op jit(solution)/shard_map/ppermute | solution.py:265
  59.7 0.0 collective-permute-done.2
  59.7 0.7 %select_select_fusion = bf16[1,16,4096]{2,1,0:T(8,128)(2,1)} fusion(bf16[1,16,4096]{2,1,0:T(8,128)(2,1)S(1)} %collective-permute-done.2, bf16[1,16,4096]{2,1,0:T(8,128)(2,1)S(1)} %collective-permute-done.3, bf16[1,16,4096]{2,1,0:T(8,128)(2,1)S(1)} %collective-permute-done.4, pred[]{:T(512)S(6)} %eq.8, pred[]{:T(512)S(6)} %eq.7), kind=kLoop, calls=%fused_computation | loop fusion | flops 131072 | bytes 524290 | tf_op jit(solution)/shard_map/jit(_where)/select_n | solution.py:282
  (4 shorter events, 0.0 us)
Async XLA Ops:
  0.6 9.6 %copy-start = (s32[1,1,64]{2,1,0:T(1,128)S(1)}, s32[1,1,64]{2,1,0:T(1,128)}, u32[]{:S(2)}) copy-start(s32[1,1,64]{2,1,0:T(1,128)} %param.14) | copy-start | bytes 772
  2.6 22.8 %all-to-all-start.2 = ((bf16[8,16,4096]{2,1,0:T(8,128)(2,1)}), bf16[8,16,4096]{2,1,0:T(8,128)(2,1)S(1)}, u32[]{:S(2)}, u32[]{:S(2)}) async-start(bf16[8,16,4096]{2,1,0:T(8,128)(2,1)} %spread.1), calls=%async_computation.2 | async-start | bytes 2097152 | tf_op jit(solution)/shard_map/all_to_all | solution.py:197
  14.6 4.3 %collective-permute-start = (s16[4,16,4224]{2,1,0:T(8,128)(2,1)S(1)}, s16[4,16,4224]{2,1,0:T(8,128)(2,1)S(1)}, u32[]{:S(2)}, u32[]{:S(2)}) collective-permute-start(s16[4,16,4224]{2,1,0:T(8,128)(2,1)S(1)} %get-tuple-element.40), channel_id=1, source_target_pairs={{0,1},{1,0},{2,3},{3,2},{4,5},{5,4},{6,7},{7,6},{8,9},{9,8},{10,11... | collective-permute-start | bytes 1622024 | tf_op jit(solution)/shard_map/ppermute | solution.py:219
  16.5 4.0 %collective-permute-start.1 = (s16[4,16,4224]{2,1,0:T(8,128)(2,1)S(1)}, s16[4,16,4224]{2,1,0:T(8,128)(2,1)S(1)}, u32[]{:S(2)}, u32[]{:S(2)}) collective-permute-start(s16[4,16,4224]{2,1,0:T(8,128)(2,1)S(1)} %get-tuple-element.41), channel_id=1, source_target_pairs={{0,1},{1,0},{2,3},{3,2},{4,5},{5,4},{6,7},{7,6},{8,9},{9,8},{10,11... | collective-permute-start | bytes 1622024 | tf_op jit(solution)/shard_map/ppermute | solution.py:219
  20.5 6.9 %copy-start.1 = (bf16[1,16,4096]{2,1,0:T(8,128)(2,1)S(1)}, bf16[1,16,4096]{2,1,0:T(8,128)(2,1)}, u32[]{:S(2)}) copy-start(bf16[1,16,4096]{2,1,0:T(8,128)(2,1)} %param.12) | copy-start | bytes 393220
  25.4 28.2 %collective-permute-start.5 = (bf16[8,16,4096]{2,1,0:T(8,128)(2,1)S(1)}, bf16[8,16,4096]{2,1,0:T(8,128)(2,1)S(1)}, u32[]{:S(2)}, u32[]{:S(2)}) collective-permute-start(bf16[8,16,4096]{2,1,0:T(8,128)(2,1)S(1)} %all-to-all-done.2.a0), channel_id=1, source_target_pairs={{0,1},{1,0},{2,3},{3,2},{4,5},{5,4},{6,7},{7,6},{8,9},{9,8},{10,11... | collective-permute-start | bytes 3145736 | tf_op jit(solution)/shard_map/ppermute | solution.py:231
  50.2 9.5 %collective-permute-start.2 = (bf16[1,16,4096]{2,1,0:T(8,128)(2,1)S(1)}, bf16[1,16,4096]{2,1,0:T(8,128)(2,1)S(1)}, u32[]{:S(2)}, u32[]{:S(2)}) collective-permute-start(bf16[1,16,4096]{2,1,0:T(8,128)(2,1)S(1)} %get-tuple-element.52), channel_id=1, source_target_pairs={{256,240},{257,241},{258,242},{259,243},{260,244},{261,245},{262,2... | collective-permute-start | bytes 393224 | tf_op jit(solution)/shard_map/ppermute | solution.py:255
  50.9 6.0 %collective-permute-start.3 = (bf16[1,16,4096]{2,1,0:T(8,128)(2,1)S(1)}, bf16[1,16,4096]{2,1,0:T(8,128)(2,1)S(1)}, u32[]{:S(2)}, u32[]{:S(2)}) collective-permute-start(bf16[1,16,4096]{2,1,0:T(8,128)(2,1)S(1)} %get-tuple-element.53), channel_id=1, source_target_pairs={{240,224},{241,225},{242,226},{243,227},{244,228},{245,229},{246,2... | collective-permute-start | bytes 393224 | tf_op jit(solution)/shard_map/ppermute | solution.py:266
  51.6 8.1 %collective-permute-start.4 = (bf16[1,16,4096]{2,1,0:T(8,128)(2,1)S(1)}, bf16[1,16,4096]{2,1,0:T(8,128)(2,1)S(1)}, u32[]{:S(2)}, u32[]{:S(2)}) collective-permute-start(bf16[1,16,4096]{2,1,0:T(8,128)(2,1)S(1)} %get-tuple-element.52), channel_id=1, source_target_pairs={{16,0},{32,16},{48,32},{64,48},{80,64},{96,80},{112,96},{128,112},... | collective-permute-start | bytes 393224 | tf_op jit(solution)/shard_map/ppermute | solution.py:265

commit v5 on v4

--- a/solution.py
+++ b/solution.py
@@ -125,7 +125,7 @@
         copy.wait()
 
 
-def total_kernel(parts, residual, out):
+def total_kernel(parts, residual, out, again):
     count, rows, width = parts.shape[0], out.shape[1], out.shape[2]
     scales = [decode_scale(parts[i, :, width:]) for i in range(count)]
     for k in range(width // BLK):
@@ -133,7 +133,7 @@
         value = jnp.zeros((rows, BLK), jnp.float32)
         for i in range(count):
             value += parts[i, :, at].astype(jnp.int32).astype(jnp.float32) * scales[i]
-        out[0, :, at] = (residual[:, at].astype(jnp.float32) + value).astype(out.dtype)
+        out[0, :, at] = again[0, :, at] = (residual[:, at].astype(jnp.float32) + value).astype(out.dtype)
 
 
 def weight_kernel(ids, counts, a0, a1, turned, out, made, sems):
@@ -238,32 +238,29 @@
         parts = lax.all_to_all(sent, "tensor", 0, 0, axis_index_groups=same_core, tiled=True)
         return pl.pallas_call(
             total_kernel,
-            out_shape=jax.ShapeDtypeStruct((1, rows, width), jnp.bfloat16),
+            out_shape=(jax.ShapeDtypeStruct((1, rows, width), jnp.bfloat16),) * 2,
             in_specs=[VMEM, VMEM],
-            out_specs=VMEM,
+            out_specs=(VMEM, VMEM),
             compiler_params=PARAMS,
             name="total",
         )(parts, residual)
 
-    early = lax.cond(
+    def nothing(sent, residual):
+        return (jnp.zeros((1, rows, width), jnp.bfloat16),) * 2
+
+    crossing, early = lax.cond(is_late, nothing, reduced, sent, residual)
+    over = lax.ppermute(crossing, "pipe", [(late + 1, late)])
+    sent, early = lax.optimization_barrier((sent, early))
+    total = lax.cond(
         is_late,
-        lambda sent, residual: jnp.zeros((1, rows, width), jnp.bfloat16),
-        reduced,
+        lambda early, sent, residual: reduced(sent, residual)[0],
+        lambda early, sent, residual: early,
+        early,
         sent,
         residual,
     )
-    over = lax.ppermute(early, "pipe", [(late + 1, late)])
-    sent, _ = lax.optimization_barrier((sent, early))
-    behind = lax.cond(
-        is_late,
-        reduced,
-        lambda sent, residual: jnp.zeros((1, rows, width), jnp.bfloat16),
-        sent,
-        residual,
-    )
-    behind, early = lax.optimization_barrier((behind, early))
-    most = lax.ppermute(early, "pipe", [(i, i - 1) for i in range(1, pipes) if i not in (late, late + 1)])
-    rest = lax.ppermute(behind, "pipe", [(late, late - 1)])
+    total, over = lax.optimization_barrier((total, over))
+    most = lax.ppermute(total, "pipe", [(i, i - 1) for i in range(1, pipes) if i != late + 1])
     grads = pl.pallas_call(
         weight_kernel,
         out_shape=jax.ShapeDtypeStruct((slots, BLK, BLK), jnp.bfloat16),
@@ -276,10 +273,9 @@
         compiler_params=PARAMS,
         cost_estimate=pl.CostEstimate(flops=4 << 30, bytes_accessed=6 << 20, transcendentals=0),
         name="weight_grads",
-    )(tile_ids[0], tile_counts, acts, lax.optimization_barrier((acts_other, behind))[0], turned)
-    rest, most, grads = lax.optimization_barrier((rest, most, grads))
-    place = lax.axis_index("pipe")
-    received = jnp.where(place == late, over, jnp.where(place == late - 1, rest, most))
+    )(tile_ids[0], tile_counts, acts, lax.optimization_barrier((acts_other, total))[0], turned)
+    most, grads = lax.optimization_barrier((most, grads))
+    received = jnp.where(is_late, over, most)
     return received, grads[None, None]
 
 

time: 60.9 us -> 61.2 us (level)
  the two profiles are of different devices: /device:TPU:96 before, /device:TPU:8 now
where the time goes in v5:
time: 61.2 us; the launch traced here: 60.9 us
  blocking collectives  22.8 us (37%)
  starting transfers between devices  14.9 us (24%)
  Pallas kernels  12.5 us (20%)
  waiting for transfers between devices  8.7 us (14%)
  between operations  1.42 us (2%)
  other arithmetic  0.67 us (1%)
    all_to_all x1, blocking collectives, reduced(): lax.all_to_all(sent, 'tensor', 0, 0, axis_index_groups=same_core, tiled=T...  22.8 us
    all_to_all x1, starting transfers between devices, shards(): lax.all_to_all(acts_copies, 'tensor', 0, 0, axis_index_groups=same_core,...  6.04 us
    pallas_call x1, Pallas kernels, shards(): pl.pallas_call(branch_kernel, out_shape=(jax.ShapeDtypeStruct((chips, row...  5.03 us
    ppermute x2, starting transfers between devices, shards(): gots = [lax.ppermute(give, 'tensor', swap) for give in gives]  4.33 us
    pallas_call x1, Pallas kernels, shards(): pl.pallas_call(weight_kernel, out_shape=jax.ShapeDtypeStruct((slots, BLK,...  3.67 us
    all_to_all x1, waiting for transfers between devices, shards(): lax.all_to_all(acts_copies, 'tensor', 0, 0, axis_index_groups=same_core,...  2.81 us
    ppermute x1, waiting for transfers between devices, shards(): over = lax.ppermute(crossing, 'pipe', [(late + 1, late)])  2.48 us
    pallas_call x1, Pallas kernels, shards(): pl.pallas_call(spread_kernel, out_shape=jax.ShapeDtypeStruct((chips, rows...  1.96 us
  transfers between devices with their start and end apart: 6, of which 4 were waited for; matrix products, arithmetic and copies ran while one was open for 0% of the time, Pallas kernels for 17%

profile of v5, /device:TPU:8, one launch (start us, length us, event | category | flops | bytes accessed | tf_op | source)
XLA Modules:
  0.0 60.9 jit_solution(15823842575712975876)
XLA Ops:
  0.6 0.0 copy-start
  0.6 2.0 %spread.1 = bf16[8,16,4096]{2,1,0:T(8,128)(2,1)} custom-call(bf16[1,16,4096]{2,1,0:T(8,128)(2,1)} %acts.1), custom_call_target="tpu_custom_call" | custom-call | tf_op jit(solution)/shard_map/spread/pallas_call | solution.py:186
  2.6 6.0 %all-to-all-start.2 = ((bf16[8,16,4096]{2,1,0:T(8,128)(2,1)}), bf16[8,16,4096]{2,1,0:T(8,128)(2,1)S(1)}, u32[]{:S(2)}, u32[]{:S(2)}) async-start(bf16[8,16,4096]{2,1,0:T(8,128)(2,1)} %spread.1), calls=%async_computation.2 | async-start | bytes 2097152 | tf_op jit(solution)/shard_map/all_to_all | solution.py:197
  9.3 0.0 copy-done
  9.3 5.0 %branch.1 = (f32[8,16,4096]{2,1,0:T(8,128)S(1)}, s16[4,16,4224]{2,1,0:T(8,128)(2,1)S(1)}, s16[4,16,4224]{2,1,0:T(8,128)(2,1)S(1)}, bf16[896,256]{1,0:T(8,128)(2,1)S(1)}) custom-call(s32[1,64]{1,0:T(1,128)S(1)} %bitcast.6, s32[1,1]{1,0:T(1,128)S(6)} %copy.14.counts, bf16[8,2,16,896]{3,2,1,0:T(8,128)(2,1)} %bitcast.11, bf16[64,128,128]{2,1,0:T(8,128)(2,1)} %bitcast.8), custom_call_target="tpu_custom_call" | custom-call | flops 1024 | bytes 1024 | tf_op jit(solution)/shard_map/branch/pallas_call | solution.py:204
  14.3 1.9 %collective-permute-start = (s16[4,16,4224]{2,1,0:T(8,128)(2,1)S(1)}, s16[4,16,4224]{2,1,0:T(8,128)(2,1)S(1)}, u32[]{:S(2)}, u32[]{:S(2)}) collective-permute-start(s16[4,16,4224]{2,1,0:T(8,128)(2,1)S(1)} %get-tuple-element.41), channel_id=1, source_target_pairs={{0,1},{1,0},{2,3},{3,2},{4,5},{5,4},{6,7},{7,6},{8,9},{9,8},{10,11... | collective-permute-start | bytes 1622024 | tf_op jit(solution)/shard_map/ppermute | solution.py:219
  16.3 2.4 %collective-permute-start.1 = (s16[4,16,4224]{2,1,0:T(8,128)(2,1)S(1)}, s16[4,16,4224]{2,1,0:T(8,128)(2,1)S(1)}, u32[]{:S(2)}, u32[]{:S(2)}) collective-permute-start(s16[4,16,4224]{2,1,0:T(8,128)(2,1)S(1)} %get-tuple-element.42), channel_id=1, source_target_pairs={{0,1},{1,0},{2,3},{3,2},{4,5},{5,4},{6,7},{7,6},{8,9},{9,8},{10,11... | collective-permute-start | bytes 1622024 | tf_op jit(solution)/shard_map/ppermute | solution.py:219
  18.7 0.0 collective-permute-done.refs_0_
  18.7 1.5 %collective-permute-done.1.refs_1_ = s16[4,16,4224]{2,1,0:T(8,128)(2,1)S(1)} collective-permute-done((s16[4,16,4224]{2,1,0:T(8,128)(2,1)S(1)}, s16[4,16,4224]{2,1,0:T(8,128)(2,1)S(1)}, u32[]{:S(2)}, u32[]{:S(2)}) %collective-permute-start.1) | collective-permute-done | bytes 540704 | tf_op jit(solution)/shard_map/ppermute | solution.py:219
  20.2 0.0 copy-start.1
  20.2 1.4 %merge.1 = s16[8,16,4224]{2,1,0:T(8,128)(2,1)} custom-call(f32[8,16,4096]{2,1,0:T(8,128)S(1)} %get-tuple-element.40.keep, s16[4,16,4224]{2,1,0:T(8,128)(2,1)S(1)} %collective-permute-done.refs_0_, s16[4,16,4224]{2,1,0:T(8,128)(2,1)S(1)} %collective-permute-done.1.refs_1_), custom_call_target="tpu_custom_call" | custom-call | flops 1024 | bytes 1024 | tf_op jit(solution)/shard_map/merge/pallas_call | solution.py:220
  21.7 2.8 %all-to-all-done.2.a0 = bf16[8,16,4096]{2,1,0:T(8,128)(2,1)S(1)} async-done(((bf16[8,16,4096]{2,1,0:T(8,128)(2,1)}), bf16[8,16,4096]{2,1,0:T(8,128)(2,1)S(1)}, u32[]{:S(2)}, u32[]{:S(2)}) %all-to-all-start.2) | async-done | bytes 1048608 | tf_op jit(solution)/shard_map/all_to_all | solution.py:197
  24.5 1.9 %collective-permute-start.4 = (bf16[8,16,4096]{2,1,0:T(8,128)(2,1)S(1)}, bf16[8,16,4096]{2,1,0:T(8,128)(2,1)S(1)}, u32[]{:S(2)}, u32[]{:S(2)}) collective-permute-start(bf16[8,16,4096]{2,1,0:T(8,128)(2,1)S(1)} %all-to-all-done.2.a0), channel_id=1, source_target_pairs={{0,1},{1,0},{2,3},{3,2},{4,5},{5,4},{6,7},{7,6},{8,9},{9,8},{10,11... | collective-permute-start | bytes 3145736 | tf_op jit(solution)/shard_map/ppermute | solution.py:231
  26.4 0.0 copy-done.1
  26.4 23.1 %conditional.2 = ((bf16[1,16,4096]{2,1,0:T(8,128)(2,1)S(1)}, bf16[1,16,4096]{2,1,0:T(8,128)(2,1)S(1)})) conditional(s32[]{:T(128)} %convert_element_type.4, (s16[8,16,4224]{2,1,0:T(8,128)(2,1)}, bf16[16,4096]{1,0:T(8,128)(2,1)S(1)}) %tuple.43, () %tuple.30), branch_computations={%region_0.0_spmd, %region_1.0_spmd} | conditional | bytes 2162696 | solution.py:251
  26.4 22.8 %all_to_all.13.parts = s16[8,16,4224]{2,1,0:T(8,128)(2,1)S(1)} all-to-all(s16[8,16,4224]{2,1,0:T(8,128)(2,1)} %get-tuple-element.12), channel_id=1, replica_groups={{0,2,4,6,8,10,12,14},{1,3,5,7,9,11,13,15},{16,18,20,22,24,26,28,30},{17..., dimensions={0} | all-to-all | bytes 2162688 | tf_op jit(solution)/shard_map/cond/branch_0_fun/all_to_all | solution.py:238
  49.2 0.3 total.2
  49.6 1.3 %collective-permute-start.2 = (bf16[1,16,4096]{2,1,0:T(8,128)(2,1)S(1)}, bf16[1,16,4096]{2,1,0:T(8,128)(2,1)S(1)}, u32[]{:S(2)}, u32[]{:S(2)}) collective-permute-start(bf16[1,16,4096]{2,1,0:T(8,128)(2,1)S(1)} %get-tuple-element.47), channel_id=1, source_target_pairs={{256,240},{257,241},{258,242},{259,243},{260,244},{261,245},{262,2... | collective-permute-start | bytes 393224 | tf_op jit(solution)/shard_map/ppermute | solution.py:252
  50.9 2.5 %collective-permute-done.2 = bf16[1,16,4096]{2,1,0:T(8,128)(2,1)S(1)} collective-permute-done((bf16[1,16,4096]{2,1,0:T(8,128)(2,1)S(1)}, bf16[1,16,4096]{2,1,0:T(8,128)(2,1)S(1)}, u32[]{:S(2)}, u32[]{:S(2)}) %collective-permute-start.2) | collective-permute-done | bytes 131104 | tf_op jit(solution)/shard_map/ppermute | solution.py:252
  53.4 1.3 %collective-permute-start.3 = (bf16[1,16,4096]{2,1,0:T(8,128)(2,1)S(1)}, bf16[1,16,4096]{2,1,0:T(8,128)(2,1)S(1)}, u32[]{:S(2)}, u32[]{:S(2)}) collective-permute-start(bf16[1,16,4096]{2,1,0:T(8,128)(2,1)S(1)} %get-tuple-element.60), channel_id=1, source_target_pairs={{16,0},{32,16},{48,32},{64,48},{80,64},{96,80},{112,96},{128,112},... | collective-permute-start | bytes 393224 | tf_op jit(solution)/shard_map/ppermute | solution.py:263
  54.7 0.0 collective-permute-done.4.a1
  54.7 3.7 %weight_grads.1 = bf16[64,128,128]{2,1,0:T(8,128)(2,1)} custom-call(s32[1,64]{1,0:T(1,128)S(1)} %bitcast.7, s32[1,1]{1,0:T(1,128)S(6)} %copy.14.counts, bf16[8,16,4096]{2,1,0:T(8,128)(2,1)S(1)} %all-to-all-done.2.a0, bf16[8,16,4096]{2,1,0:T(8,128)(2,1)S(1)} %collective-permute-done.4.a1, bf16[896,256]{1,0:T(8,128)(2,1)S(1)} %get-tuple-element.52.turned), custom_call_target="tpu_custom_call" | custom-call | flops 4294967296 | bytes 6291456 | tf_op jit(solution)/shard_map/weight_grads/pallas_call | solution.py:264
  58.4 1.9 %collective-permute-done.3 = bf16[1,16,4096]{2,1,0:T(8,128)(2,1)S(1)} collective-permute-done((bf16[1,16,4096]{2,1,0:T(8,128)(2,1)S(1)}, bf16[1,16,4096]{2,1,0:T(8,128)(2,1)S(1)}, u32[]{:S(2)}, u32[]{:S(2)}) %collective-permute-start.3) | collective-permute-done | bytes 131104 | tf_op jit(solution)/shard_map/ppermute | solution.py:263
  60.2 0.7 %broadcast_select_fusion = bf16[1,16,4096]{2,1,0:T(8,128)(2,1)} fusion(bf16[1,16,4096]{2,1,0:T(8,128)(2,1)S(1)} %collective-permute-done.2, bf16[1,16,4096]{2,1,0:T(8,128)(2,1)S(1)} %collective-permute-done.3, pred[]{:T(512)S(6)} %eq.3), kind=kLoop, calls=%fused_computation | loop fusion | flops 65536 | bytes 393217 | tf_op jit(solution)/shard_map/jit(_where)/select_n | solution.py:278
  (1 shorter events, 0.0 us)
Async XLA Ops:
  0.6 8.7 %copy-start = (s32[1,1,64]{2,1,0:T(1,128)S(1)}, s32[1,1,64]{2,1,0:T(1,128)}, u32[]{:S(2)}) copy-start(s32[1,1,64]{2,1,0:T(1,128)} %param.14) | copy-start | bytes 772
  2.6 21.9 %all-to-all-start.2 = ((bf16[8,16,4096]{2,1,0:T(8,128)(2,1)}), bf16[8,16,4096]{2,1,0:T(8,128)(2,1)S(1)}, u32[]{:S(2)}, u32[]{:S(2)}) async-start(bf16[8,16,4096]{2,1,0:T(8,128)(2,1)} %spread.1), calls=%async_computation.2 | async-start | bytes 2097152 | tf_op jit(solution)/shard_map/all_to_all | solution.py:197
  14.3 4.3 %collective-permute-start = (s16[4,16,4224]{2,1,0:T(8,128)(2,1)S(1)}, s16[4,16,4224]{2,1,0:T(8,128)(2,1)S(1)}, u32[]{:S(2)}, u32[]{:S(2)}) collective-permute-start(s16[4,16,4224]{2,1,0:T(8,128)(2,1)S(1)} %get-tuple-element.41), channel_id=1, source_target_pairs={{0,1},{1,0},{2,3},{3,2},{4,5},{5,4},{6,7},{7,6},{8,9},{9,8},{10,11... | collective-permute-start | bytes 1622024 | tf_op jit(solution)/shard_map/ppermute | solution.py:219
  16.3 4.0 %collective-permute-start.1 = (s16[4,16,4224]{2,1,0:T(8,128)(2,1)S(1)}, s16[4,16,4224]{2,1,0:T(8,128)(2,1)S(1)}, u32[]{:S(2)}, u32[]{:S(2)}) collective-permute-start(s16[4,16,4224]{2,1,0:T(8,128)(2,1)S(1)} %get-tuple-element.42), channel_id=1, source_target_pairs={{0,1},{1,0},{2,3},{3,2},{4,5},{5,4},{6,7},{7,6},{8,9},{9,8},{10,11... | collective-permute-start | bytes 1622024 | tf_op jit(solution)/shard_map/ppermute | solution.py:219
  20.2 6.2 %copy-start.1 = (bf16[1,16,4096]{2,1,0:T(8,128)(2,1)S(1)}, bf16[1,16,4096]{2,1,0:T(8,128)(2,1)}, u32[]{:S(2)}) copy-start(bf16[1,16,4096]{2,1,0:T(8,128)(2,1)} %param.12) | copy-start | bytes 393220
  24.5 30.2 %collective-permute-start.4 = (bf16[8,16,4096]{2,1,0:T(8,128)(2,1)S(1)}, bf16[8,16,4096]{2,1,0:T(8,128)(2,1)S(1)}, u32[]{:S(2)}, u32[]{:S(2)}) collective-permute-start(bf16[8,16,4096]{2,1,0:T(8,128)(2,1)S(1)} %all-to-all-done.2.a0), channel_id=1, source_target_pairs={{0,1},{1,0},{2,3},{3,2},{4,5},{5,4},{6,7},{7,6},{8,9},{9,8},{10,11... | collective-permute-start | bytes 3145736 | tf_op jit(solution)/shard_map/ppermute | solution.py:231
  49.6 3.8 %collective-permute-start.2 = (bf16[1,16,4096]{2,1,0:T(8,128)(2,1)S(1)}, bf16[1,16,4096]{2,1,0:T(8,128)(2,1)S(1)}, u32[]{:S(2)}, u32[]{:S(2)}) collective-permute-start(bf16[1,16,4096]{2,1,0:T(8,128)(2,1)S(1)} %get-tuple-element.47), channel_id=1, source_target_pairs={{256,240},{257,241},{258,242},{259,243},{260,244},{261,245},{262,2... | collective-permute-start | bytes 393224 | tf_op jit(solution)/shard_map/ppermute | solution.py:252
  53.4 6.8 %collective-permute-start.3 = (bf16[1,16,4096]{2,1,0:T(8,128)(2,1)S(1)}, bf16[1,16,4096]{2,1,0:T(8,128)(2,1)S(1)}, u32[]{:S(2)}, u32[]{:S(2)}) collective-permute-start(bf16[1,16,4096]{2,1,0:T(8,128)(2,1)S(1)} %get-tuple-element.60), channel_id=1, source_target_pairs={{16,0},{32,16},{48,32},{64,48},{80,64},{96,80},{112,96},{128,112},... | collective-permute-start | bytes 393224 | tf_op jit(solution)/shard_map/ppermute | solution.py:263
